TPU v7x, 32 devices: a whole 2x2x4 slice. The times are simulated.
32 devices in a mesh: dp: 4 (over z), seq: 8 (over y, x, core).
Axes of the slice: x: 2, y: 2, z: 4, core: 2. Of those that a mesh axis runs over, the one named last changes fastest.
Arguments:
- tokens: bfloat16 [4, 16384, 2048], P('dp', 'seq'), may hold values from -6 to 6
- gate: bfloat16 [4, 16384, 2048], P('dp', 'seq'), may hold values from -6 to 6
- cotangent: bfloat16 [4, 16384, 2048], P('dp', 'seq'), may hold values from -6 to 6
- first_factor: bfloat16 [32, 512, 512], P('seq'), may hold values from -0.25 to 0.25
- second_factor: bfloat16 [512, 32, 32], P('seq'), may hold values from -1 to 1
Outputs:
- input_grad: bfloat16 [4, 16384, 2048], P('dp', 'seq')
- gate_grad: bfloat16 [4, 16384, 2048], P('dp', 'seq')
- first_grad: float32 [32, 512, 512], P('seq', 'dp')
- second_grad: float32 [512, 32, 32], P('seq', 'dp')
All inputs are finite; a program needn't handle non-finite values.
Results may differ from a plain program's by a relative error of at most 0.0057.
Values may be sent and summed in bfloat16 or wider, within the bound.
No kernel may reach another device: no remote copies, remote signals or barrier semaphores. Data moves between devices by JAX's collectives and lax.ppermute only.
A program may use at most 128 MiB of HBM per device.

v0:
```python
import jax
import jax.numpy as jnp
from jax import lax
from jax.sharding import PartitionSpec as P


def local(tokens, gate, cotangent, first_factor, second_factor):
    seqs, rows, width = tokens.shape
    dp_count = lax.axis_size("dp")
    local_blocks, block = (first_factor.shape[0], first_factor.shape[1])
    local_offsets, nblocks = (second_factor.shape[0], second_factor.shape[1])
    factor = 1.0 / jnp.sqrt(jnp.float32(width * seqs * dp_count))
    blocks = tokens.reshape(seqs, local_blocks, block, width)
    hidden = jnp.einsum(
        "bij,nbjc->nbic", first_factor, blocks, preferred_element_type=jnp.float32
    ).astype(jnp.bfloat16)
    hidden_t = lax.all_to_all(hidden, "seq", split_axis=2, concat_axis=1, tiled=True)
    mixed = jnp.einsum(
        "ipb,nbic->nipc", second_factor, hidden_t, preferred_element_type=jnp.float32
    )
    hidden_t, mixed = (hidden_t, mixed)
    gate_t = gate.reshape(seqs, local_offsets, nblocks, width).astype(jnp.float32)
    cot_t = cotangent.reshape(seqs, local_offsets, nblocks, width).astype(jnp.float32)
    gate_grad = (cot_t * mixed).astype(jnp.bfloat16).reshape(seqs, rows, width)
    mixed_grad = (cot_t * gate_t).astype(jnp.bfloat16)
    second_terms = (
        jnp.einsum("nipc,nbic->ipb", mixed_grad, hidden_t, preferred_element_type=jnp.float32)
        * factor
    )
    hidden_grad_t = jnp.einsum(
        "ipb,nipc->nbic", second_factor, mixed_grad, preferred_element_type=jnp.float32
    ).astype(jnp.bfloat16)
    second_share = lax.psum_scatter(second_terms, "dp", scatter_dimension=1, tiled=True)
    hidden_grad = lax.all_to_all(hidden_grad_t, "seq", split_axis=1, concat_axis=2, tiled=True)
    input_grad = jnp.einsum(
        "bij,nbic->nbjc", first_factor, hidden_grad, preferred_element_type=jnp.float32
    ).astype(jnp.bfloat16)
    hidden_grad, input_grad = (hidden_grad, input_grad)
    first_terms = (
        jnp.einsum("nbic,nbjc->bij", hidden_grad, blocks, preferred_element_type=jnp.float32)
        * factor
    )
    first_share = lax.psum_scatter(first_terms, "dp", scatter_dimension=1, tiled=True)
    return (input_grad.reshape(seqs, rows, width), gate_grad, first_share, second_share)


def solution(mesh):
    placed = (
        P("dp", "seq", None),
        P("dp", "seq", None),
        P("dp", "seq", None),
        P("seq", None, None),
        P("seq", None, None),
    )
    return jax.shard_map(
        local,
        mesh=mesh,
        in_specs=placed,
        out_specs=(
            P("dp", "seq", None),
            P("dp", "seq", None),
            P("seq", "dp", None),
            P("seq", "dp", None),
        ),
        check_vma=False,
    )
```

profile of v0, /device:TPU:0, one launch (start us, length us, event | category | flops | bytes accessed | tf_op | source)
XLA Modules:
  0.0 338.6 jit_solution(7417421566425779159)
XLA Ops:
  7.2 0.0 copy-start
  7.2 1.6 copy-done
  8.8 11.5 %convert_bitcast_fusion = bf16[1,4,512,2048]{2,3,1,0:T(8,128)(2,1)} fusion(bf16[4,512,2048]{2,1,0:T(8,128)(2,1)} %bitcast.52, bf16[4,512,512]{2,1,0:T(8,128)(2,1)S(1)} %copy-done), kind=kOutput, calls=%fused_computation.3 | convolution fusion | flops 4299161600 | bytes 18874368 | tf_op jit(solution)/shard_map/bij,nbjc->nbic/dot_general | solution.py:14
  20.2 14.9 %copy.29 = bf16[1,4,512,2048]{3,1,0,2:T(4,128)(2,1)} copy(bf16[1,4,512,2048]{2,3,1,0:T(8,128)(2,1)} %convert_bitcast_fusion) | data formatting | bytes 16777216 | tf_op jit(solution)/shard_map/convert_element_type | solution.py:16
  35.2 0.0 copy-start.2
  35.2 5.3 %all-to-all-start.1 = ((bf16[1,4,512,2048]{3,1,0,2:T(4,128)(2,1)}), bf16[1,4,512,2048]{3,1,0,2:T(4,128)(2,1)}, u32[]{:S(2)}, u32[]{:S(2)}) async-start(bf16[1,4,512,2048]{3,1,0,2:T(4,128)(2,1)} %copy.29), calls=%async_computation.1 | async-start | bytes 16777216 | tf_op jit(solution)/shard_map/all_to_all | solution.py:17
  40.5 0.0 copy-done.2
  40.5 0.8 copy.32
  41.3 7.5 %multiply_convert_fusion = bf16[1,2048,2048]{2,1,0:T(8,128)(2,1)S(1)} fusion(bf16[1,2048,2048]{2,1,0:T(8,128)(2,1)} %param.6, bf16[1,2048,2048]{2,1,0:T(8,128)(2,1)} %param.7), kind=kLoop, calls=%fused_computation.2 | loop fusion | flops 16777216 | bytes 25165824 | tf_op jit(solution)/shard_map/convert_element_type | solution.py:25
  48.8 0.0 copy-start.1
  48.8 3.2 copy-done.1
  52.0 4.7 %convert_bitcast_fusion.1 = bf16[1,32,64,2048]{3,1,2,0:T(8,128)(2,1)} fusion(bf16[64,32,32]{2,1,0:T(8,128)(2,1)S(1)} %copy.32, bf16[64,32,2048]{2,1,0:T(8,128)(2,1)S(1)} %bitcast.45), kind=kOutput, calls=%fused_computation.4 | convolution fusion | flops 272629760 | bytes 16908288 | tf_op jit(solution)/shard_map/ipb,nipc->nbic/dot_general | solution.py:30
  56.7 11.4 %copy.25 = bf16[1,32,64,2048]{3,2,0,1:T(8,128)(2,1)} copy(bf16[1,32,64,2048]{3,1,2,0:T(8,128)(2,1)} %convert_bitcast_fusion.1) | data formatting | bytes 16777216 | tf_op jit(solution)/shard_map/convert_element_type | solution.py:32
  68.1 66.9 %all-to-all-done.1 = bf16[1,4,512,2048]{3,1,0,2:T(4,128)(2,1)} async-done(((bf16[1,4,512,2048]{3,1,0,2:T(4,128)(2,1)}), bf16[1,4,512,2048]{3,1,0,2:T(4,128)(2,1)}, u32[]{:S(2)}, u32[]{:S(2)}) %all-to-all-start.1) | async-done | bytes 8388640 | tf_op jit(solution)/shard_map/all_to_all | solution.py:17
  135.0 4.9 %all-to-all-start = ((bf16[1,32,64,2048]{3,2,0,1:T(8,128)(2,1)}), bf16[1,32,64,2048]{3,2,0,1:T(8,128)(2,1)}, u32[]{:S(2)}, u32[]{:S(2)}) async-start(bf16[1,32,64,2048]{3,2,0,1:T(8,128)(2,1)} %copy.25), calls=%async_computation | async-start | bytes 16777216 | tf_op jit(solution)/shard_map/all_to_all | solution.py:34
  139.9 0.2 reduce-scatter.5.cloned.1.call-start
  140.2 11.4 %copy.30 = bf16[1,4,512,2048]{3,2,1,0:T(8,128)(2,1)} copy(bf16[1,4,512,2048]{3,1,0,2:T(4,128)(2,1)} %all-to-all-done.1) | data formatting | bytes 16777216 | tf_op jit(solution)/shard_map/all_to_all | solution.py:17
  151.6 12.1 %copy.31 = bf16[1,8,4,64,2048]{4,2,1,3,0:T(4,128)(2,1)} copy(bf16[1,8,4,64,2048]{4,3,1,2,0:T(8,128)(2,1)} %bitcast.48) | data formatting | bytes 16777216 | tf_op jit(solution)/shard_map/all_to_all | solution.py:17
  163.7 12.5 %reshape.75 = bf16[32,64,2048]{2,0,1:T(8,128)(2,1)} reshape(bf16[1,8,4,64,2048]{4,2,1,3,0:T(4,128)(2,1)} %copy.31) | data formatting | bytes 16777216 | tf_op jit(solution)/shard_map/reshape.11
  176.1 9.1 %convolution_multiply_fusion.1 = f32[64,32,32]{2,1,0:T(8,128)} fusion(bf16[64,32,2048]{2,1,0:T(8,128)(2,1)} %bitcast.46, bf16[32,64,2048]{2,0,1:T(8,128)(2,1)} %reshape.75), kind=kOutput, calls=%fused_computation.7 | convolution fusion | flops 268500992 | bytes 17039360 | tf_op jit(solution)/shard_map/nipc,nbic->ipb/dot_general | solution.py:27
  185.3 0.0 reduce-scatter.5.cloned.1.call-update
  185.3 0.3 reduce-scatter.3.cloned.1.call-start
  185.6 48.4 %all-to-all-done = bf16[1,32,64,2048]{3,2,0,1:T(8,128)(2,1)} async-done(((bf16[1,32,64,2048]{3,2,0,1:T(8,128)(2,1)}), bf16[1,32,64,2048]{3,2,0,1:T(8,128)(2,1)}, u32[]{:S(2)}, u32[]{:S(2)}) %all-to-all-start) | async-done | bytes 8388640 | tf_op jit(solution)/shard_map/all_to_all | solution.py:34
  234.0 8.3 %copy.26 = bf16[1,8,4,64,2048]{4,3,1,2,0:T(8,128)(2,1)} copy(bf16[1,8,4,64,2048]{4,3,2,1,0:T(8,128)(2,1)} %bitcast.3) | data formatting | bytes 16777216 | tf_op jit(solution)/shard_map/all_to_all | solution.py:34
  242.3 12.2 %convolution_multiply_fusion = f32[4,512,512]{2,1,0:T(8,128)} fusion(bf16[4,512,2048]{2,1,0:T(8,128)(2,1)} %bitcast.50, bf16[4,512,2048]{2,1,0:T(8,128)(2,1)} %bitcast.53), kind=kOutput, calls=%fused_computation.6 | convolution fusion | flops 4296015872 | bytes 20971520 | tf_op jit(solution)/shard_map/nbic,nbjc->bij/dot_general | solution.py:40
  254.5 0.0 reduce-scatter.3.cloned.1.call-update
  254.5 11.5 %fusion = bf16[1,64,32,2048]{3,2,1,0:T(8,128)(2,1)} fusion(bf16[64,32,32]{2,1,0:T(8,128)(2,1)S(1)} %copy.32, bf16[32,64,2048]{2,0,1:T(8,128)(2,1)} %reshape.75, bf16[1,64,32,2048]{3,2,1,0:T(8,128)(2,1)} %bitcast.47), kind=kOutput, calls=%fused_computation.1 | convolution fusion | flops 281018368 | bytes 25296896 | tf_op jit(solution)/shard_map/ipb,nbic->nipc/dot_general | solution.py:18
  266.0 10.2 %convolution_convert_fusion = bf16[4,2048,512]{1,2,0:T(8,128)(2,1)} fusion(bf16[4,512,2048]{2,1,0:T(8,128)(2,1)} %bitcast.51, bf16[4,512,512]{2,1,0:T(8,128)(2,1)S(1)} %copy-done), kind=kOutput, calls=%fused_computation.5 | convolution fusion | flops 4299161600 | bytes 18874368 | tf_op jit(solution)/shard_map/bij,nbic->nbjc/dot_general | solution.py:35
  276.2 0.0 reduce-scatter.5.cloned.1.call-done
  276.2 1.7 copy.33
  278.0 53.8 %reduce-scatter.3.cloned.1.call-done = f32[4,128,512]{2,1,0:T(8,128)} async-done(((f32[4,512,512]{2,1,0:T(8,128)}), f32[4,128,512]{2,1,0:T(8,128)}) %reduce-scatter.3.cloned.1.call-update) | async-done | bytes 1048592 | tf_op jit(solution)/shard_map/reduce_scatter | solution.py:43
Async XLA Ops:
  7.2 1.6 copy-start
  35.2 5.3 %copy-start.2 = (bf16[64,32,32]{0,2,1:T(8,128)(2,1)S(1)}, bf16[64,32,32]{0,2,1:T(8,128)(2,1)}, u32[]{:S(2)}) copy-start(bf16[64,32,32]{0,2,1:T(8,128)(2,1)} %param.9) | copy-start | bytes 393220
  35.2 99.8 %all-to-all-start.1 = ((bf16[1,4,512,2048]{3,1,0,2:T(4,128)(2,1)}), bf16[1,4,512,2048]{3,1,0,2:T(4,128)(2,1)}, u32[]{:S(2)}, u32[]{:S(2)}) async-start(bf16[1,4,512,2048]{3,1,0,2:T(4,128)(2,1)} %copy.29), calls=%async_computation.1 | async-start | bytes 16777216 | tf_op jit(solution)/shard_map/all_to_all | solution.py:17
  48.8 3.2 copy-start.1
  135.0 99.0 %all-to-all-start = ((bf16[1,32,64,2048]{3,2,0,1:T(8,128)(2,1)}), bf16[1,32,64,2048]{3,2,0,1:T(8,128)(2,1)}, u32[]{:S(2)}, u32[]{:S(2)}) async-start(bf16[1,32,64,2048]{3,2,0,1:T(8,128)(2,1)} %copy.25), calls=%async_computation | async-start | bytes 16777216 | tf_op jit(solution)/shard_map/all_to_all | solution.py:34
  139.9 136.3 %reduce-scatter.5.cloned.1.call-start = ((), (), s32[]{:S(2)}) async-start(), calls=%async_computation.5 | async-start | bytes 1310720 | tf_op jit(solution)/shard_map/reduce_scatter | solution.py:33
  185.3 146.4 %reduce-scatter.3.cloned.1.call-start = ((), (), s32[]{:S(2)}) async-start(), calls=%async_computation.4 | async-start | bytes 5242880 | tf_op jit(solution)/shard_map/reduce_scatter | solution.py:43
Sparse Core Ops, SparseCore 0:
  185.4 29.4 reduce-scatter.4
  254.7 77.0 reduce-scatter.2
where the time goes:
time: 340 us; the launch traced here: 339 us
  waiting for transfers between devices  169 us (50%)
  local copies, waits for them, and re-layouts  77.9 us (23%)
  matrix products  59.2 us (17%)
  between operations  14.1 us (4%)
  starting transfers between devices  10.7 us (3%)
  other arithmetic  7.51 us (2%)
    all_to_all x1, waiting for transfers between devices, local(): lax.all_to_all(hidden, 'seq', split_axis=2, concat_axis=1, tiled=True)  66.9 us
    reduce_scatter x1, waiting for transfers between devices, local(): lax.psum_scatter(first_terms, 'dp', scatter_dimension=1, tiled=True)  53.8 us
    all_to_all x1, waiting for transfers between devices, local(): lax.all_to_all(hidden_grad_t, 'seq', split_axis=1, concat_axis=2, tiled=T...  48.4 us
    all_to_all x2, local copies, waits for them, and re-layouts, local(): lax.all_to_all(hidden, 'seq', split_axis=2, concat_axis=1, tiled=True)  23.5 us
    convert_element_type x1, local copies, waits for them, and re-layouts, local(): hidden = jnp.einsum('bij,nbjc->nbic', first_factor, blocks, preferred_ele...  14.9 us
    another operation x1, local copies, waits for them, and re-layouts  12.5 us
    dot_general x1, matrix products, local(): jnp.einsum('nbic,nbjc->bij', hidden_grad, blocks, preferred_element_type=...  12.2 us
    dot_general x1, matrix products, local(): jnp.einsum('ipb,nbic->nipc', second_factor, hidden_t, preferred_element_t...  11.5 us
  transfers between devices with their start and end apart: 4, of which 3 were waited for; matrix products, arithmetic and copies ran while one was open for 34% of the time, Pallas kernels for 0%

commit v1 on v0

v1 whole, which is shorter than its diff:
```python
import functools

import jax
import jax.numpy as jnp
from jax import lax
from jax.experimental import pallas as pl
from jax.experimental.pallas import tpu as pltpu
from jax.sharding import PartitionSpec as P

F32, BF16 = jnp.float32, jnp.bfloat16
G = 8
T = 2 * G
VMEM_LIMIT = 60 * 1024 * 1024
NT = (((1,), (1,)), ((), ()))
ANY = pl.BlockSpec(memory_space=pl.ANY)


def _dot(a, b):
    return jnp.dot(a, b, preferred_element_type=F32)


def _dot_nt(a, b):
    return lax.dot_general(a, b, NT, preferred_element_type=F32)


def _iota(shape, dim):
    return lax.broadcasted_iota(jnp.int32, shape, dim)


def _call(kernel, grid, in_specs, out_specs, out_shape, scratch, flops, nbytes, name, after=(), aliases=None):
    return pl.pallas_call(
        kernel,
        grid_spec=pltpu.PrefetchScalarGridSpec(
            num_scalar_prefetch=1,
            grid=grid,
            in_specs=list(in_specs) + [ANY] * len(after),
            out_specs=out_specs,
            scratch_shapes=scratch,
        ),
        out_shape=out_shape,
        input_output_aliases=aliases or {},
        compiler_params=pltpu.CompilerParams(vmem_limit_bytes=VMEM_LIMIT),
        cost_estimate=pl.CostEstimate(flops=flops, bytes_accessed=nbytes, transcendentals=0),
        name=name,
    )


def _pick(nb, lb, flip):
    block = _iota((nb * G, nb), 0) // G
    block = jnp.bitwise_xor(block // lb, flip) * lb + block % lb
    return (block == _iota((nb * G, nb), 1)).astype(BF16)


def hidden_grad_kernel(nseq, lb, nb, split, me_ref, s_ref, gate_ref, cot_ref, *rest):
    outs, (pick, mask, mt, res) = rest[-4 - (nseq if split else 1):-4], rest[-4:]
    rows, cols = nb * G, G * nb
    width = gate_ref.shape[2]

    @pl.when(pl.program_id(0) == 0)
    def _():
        pick[...] = _pick(nb, lb, me_ref[0] if split else 0)
        same = _iota((rows, cols), 0) % G == _iota((rows, cols), 1) // nb
        mask[...] = same.astype(F32)

    mt[...] = (_dot_nt(pick[...], s_ref[...]) * mask[...]).astype(BF16)
    for c in range(0, width, 256):
        mg = cot_ref[0, :, c:c + 256] * gate_ref[0, :, c:c + 256]
        res[:, c:c + 256] = _dot(mt[...], mg).astype(BF16)
    if split:
        for k in range(nseq):
            outs[k][...] = res[k * lb * G:(k + 1) * lb * G, :].reshape(outs[k].shape)
    else:
        outs[0][...] = res[...].reshape(outs[0].shape)


def hidden_grad(me, s2, gate, cot, after, g0, ng, split, nseq, lb, nb):
    width = gate.shape[2]
    rows = pl.BlockSpec((1, G * nb, width), lambda g, m: (0, g0 + g, 0))
    if split:
        out_specs = [pl.BlockSpec((lb // 2, 1, T, width), lambda g, m: (0, g, 0, 0))] * nseq
        out_shape = [jax.ShapeDtypeStruct((lb // 2, ng, T, width), BF16)] * nseq
    else:
        out_specs = pl.BlockSpec((nseq, lb // 2, 1, T, width), lambda g, m: (0, 0, g, 0, 0))
        out_shape = jax.ShapeDtypeStruct((nseq, lb // 2, ng, T, width), BF16)
    return _call(
        functools.partial(hidden_grad_kernel, nseq, lb, nb, split),
        (ng,),
        [pl.BlockSpec((G * nb, nb), lambda g, m: (g0 + g, 0)), rows, rows],
        out_specs,
        out_shape,
        [
            pltpu.VMEM((nb * G, nb), BF16),
            pltpu.VMEM((nb * G, G * nb), F32),
            pltpu.VMEM((nb * G, G * nb), BF16),
            pltpu.VMEM((nb * G, width), BF16),
        ],
        2 * ng * (G * nb) ** 2 * width,
        6 * ng * G * nb * width,
        "hidden_grad",
        after,
    )(me, s2, gate, cot, *after)


def hidden_kernel(nseq, lo, spans, me_ref, f_ref, x_ref, *rest):
    outs, fp = rest[-1 - nseq * len(spans):-1], rest[-1]
    block = f_ref.shape[1]
    width = x_ref.shape[2]

    @pl.when(pl.program_id(1) == 0)
    def _():
        for b in range(2):
            for k in range(nseq):
                start = pl.multiple_of(jnp.bitwise_xor(me_ref[0], k) * lo, lo)
                fp[b, k * lo:(k + 1) * lo, :] = f_ref[b, pl.ds(start, lo), :]

    both = [
        _dot(fp[b], x_ref[0, b * block:(b + 1) * block, :]).reshape(nseq, lo // G, 1, G, width)
        for b in range(2)
    ]
    res = jnp.concatenate(both, axis=2).reshape(nseq, lo // G, T, width).astype(BF16)
    for j, (g0, ng) in enumerate(spans):
        for k in range(nseq):
            outs[j * nseq + k][0] = res[k, g0:g0 + ng]


def hidden_forward(me, f, x, after, spans, nseq, lo, cb):
    lb, block, _ = f.shape
    width = x.shape[2]
    out_specs, out_shape = [], []
    for _, ng in spans:
        out_specs += [pl.BlockSpec((1, ng, T, cb), lambda b, c, m: (b, 0, 0, c))] * nseq
        out_shape += [jax.ShapeDtypeStruct((lb // 2, ng, T, width), BF16)] * nseq
    outs = _call(
        functools.partial(hidden_kernel, nseq, lo, spans),
        (lb // 2, width // cb),
        [
            pl.BlockSpec((2, block, block), lambda b, c, m: (b, 0, 0)),
            pl.BlockSpec((1, 2 * block, cb), lambda b, c, m: (0, b, c)),
        ],
        out_specs,
        out_shape,
        [pltpu.VMEM((2, block, block), BF16)],
        2 * lb * block * block * width,
        4 * lb * block * width,
        "hidden",
        after,
    )(me, f, x, *after)
    return [list(outs[j * nseq:(j + 1) * nseq]) for j in range(len(spans))]


def block_grads_kernel(nseq, ndp, lo, factor, me_ref, f_ref, x_ref, hg_ref, *rest):
    hgs = dict(zip([0] + _wire_order(nseq), rest[:nseq]))
    dx_ref, kept, sent, ft, grad, acc = rest[-6:]
    c = pl.program_id(1)
    block = f_ref.shape[1]
    width = x_ref.shape[2]

    @pl.when(c == 0)
    def _():
        for b in range(2):
            ft[b] = f_ref[b].T
        acc[...] = jnp.zeros_like(acc)

    def unpack(packed, source, first):
        ng = packed.shape[0]
        wide = packed.astype(F32).reshape(ng, 2, G, width)
        for b in range(2):
            part = wide[:, b].reshape(ng * G, width).astype(BF16)
            grad[b, source, first:first + ng * G, :] = part

    early = hg_ref.shape[2]
    for k in range(nseq):
        unpack(hg_ref[k, 0], k, 0)
        unpack(hgs[k][0], jnp.bitwise_xor(me_ref[0], k), early * G)
    for b in range(2):
        hg = grad[b].reshape(block, width)
        rows = slice(b * block, (b + 1) * block)
        dx_ref[0, rows, :] = _dot(ft[b], hg).astype(BF16)
        acc[b] += _dot_nt(hg, x_ref[0, rows, :])

    @pl.when(c == pl.num_programs(1) - 1)
    def _():
        share = block // ndp
        for slot in range(ndp):
            start = pl.multiple_of(jnp.bitwise_xor(me_ref[1], slot) * share, share)
            part = acc[:, pl.ds(start, share), :] * factor
            to = sent if slot % 2 else kept
            to[slot // 2] = part.astype(to.dtype)


def block_grads(me, f, x, hg, hgs, after, nseq, ndp, factor, cb):
    lb, block, _ = f.shape
    width = x.shape[2]
    share = block // ndp
    lo = block // nseq
    rows = pl.BlockSpec((1, 2 * block, cb), lambda b, c, m: (0, b, c))
    return _call(
        functools.partial(block_grads_kernel, nseq, ndp, lo, factor),
        (lb // 2, width // cb),
        [
            pl.BlockSpec((2, block, block), lambda b, c, m: (b, 0, 0)),
            rows,
            pl.BlockSpec((nseq, 1, hg.shape[2], T, cb), lambda b, c, m: (0, b, 0, 0, c)),
        ]
        + [pl.BlockSpec((1, hgs[0].shape[1], T, cb), lambda b, c, m: (b, 0, 0, c))] * nseq,
        [rows] + [pl.BlockSpec((ndp // 2, 2, share, block), lambda b, c, m: (0, b, 0, 0))] * 2,
        [
            jax.ShapeDtypeStruct(x.shape, BF16),
            jax.ShapeDtypeStruct((ndp // 2, lb, share, block), F32),
            jax.ShapeDtypeStruct((ndp // 2, lb, share, block), BF16),
        ],
        [
            pltpu.VMEM((2, block, block), BF16),
            pltpu.VMEM((2, nseq, lo, cb), BF16),
            pltpu.VMEM((2, block, block), F32),
        ],
        4 * lb * block * block * width,
        6 * lb * block * width,
        "block_grads",
        after,
    )(me, f, x, hg, *[hgs[k] for k in [0] + _wire_order(nseq)], *after)


def mixed_kernel(nseq, ndp, lb, nb, factor, me_ref, s_ref, gate_ref, cot_ref, *rest):
    hs = dict(zip([0] + _wire_order(nseq), rest[:nseq]))
    gg_ref, out, pick, mask, order, choose, m, hid, mg = rest[-9:]
    rows, cols = nb * G, G * nb
    share = nb // ndp
    width = gg_ref.shape[2]

    @pl.when(pl.program_id(0) == 0)
    def _():
        pick[...] = _pick(nb, lb, me_ref[0])
        same = _iota((cols, rows), 1) % G == _iota((cols, rows), 0) // nb
        mask[...] = same.astype(F32)
        r = _iota((nb, nb), 1)
        block = jnp.bitwise_xor(r // lb, me_ref[0]) * lb + r % lb
        order[...] = (block == _iota((nb, nb), 0)).astype(BF16)
        q = _iota((cols, cols), 1)
        choose[...] = (_iota((cols, cols), 0) == (q % G) * nb + q // G).astype(BF16)

    m[...] = (_dot_nt(s_ref[...], pick[...]) * mask[...]).astype(BF16)
    for k in range(nseq):
        hid[k * lb * G:(k + 1) * lb * G, :] = hs[k][...].reshape(lb * G, width)
    for c in range(0, width, 256):
        cot = cot_ref[0, :, c:c + 256]
        mixed = _dot(m[...], hid[:, c:c + 256])
        gg_ref[0, :, c:c + 256] = (cot.astype(F32) * mixed).astype(BF16)
        mg[:, c:c + 256] = cot * gate_ref[0, :, c:c + 256]
    kept = _dot_nt(mg[...], hid[...]) * mask[...]
    terms = jnp.sum(kept.T.reshape(nb, G, cols), axis=1) * factor
    terms = _dot(order[...], terms.astype(BF16)).astype(BF16)
    terms = _dot(terms, choose[...])
    tall = out.shape[2]
    for z in range(ndp):
        part = terms[:, z * share * G:(z + 1) * share * G]
        part = [part[r:r + tall] for r in range(0, nb, tall)]
        out[z, 0] = jnp.concatenate(part, axis=1).astype(BF16)


def mixed_stage(me, s2, gate, cot, hs, prev, after, g0, ng, groups, nseq, ndp, lb, nb, factor):
    width = gate.shape[2]
    rows = pl.BlockSpec((1, G * nb, width), lambda g, m: (0, g0 + g, 0))
    share = nb // ndp
    extra = list(prev) + list(after)
    square = (G * nb, nb * G)
    wide = max(128, share * G)
    tall = nb * share * G // wide
    return _call(
        functools.partial(mixed_kernel, nseq, ndp, lb, nb, factor),
        (ng,),
        [pl.BlockSpec((G * nb, nb), lambda g, m: (g0 + g, 0)), rows, rows]
        + [pl.BlockSpec((lb // 2, 1, T, width), lambda g, m: (0, g, 0, 0))] * nseq,
        [rows, pl.BlockSpec((ndp, 1, tall, wide), lambda g, m: (0, g0 + g, 0, 0))],
        [
            jax.ShapeDtypeStruct(gate.shape, BF16),
            jax.ShapeDtypeStruct((ndp, groups, tall, wide), BF16),
        ],
        [
            pltpu.VMEM((nb * G, nb), BF16),
            pltpu.VMEM(square, F32),
            pltpu.VMEM((nb, nb), BF16),
            pltpu.VMEM((G * nb, G * nb), BF16),
            pltpu.VMEM(square, BF16),
            pltpu.VMEM((nb * G, width), BF16),
            pltpu.VMEM((G * nb, width), BF16),
        ],
        4 * ng * (G * nb) ** 2 * width,
        8 * ng * G * nb * width,
        "mixed",
        extra,
        {4 + nseq + i: i for i in range(len(prev))},
    )(me, s2, gate, cot, *[hs[k] for k in [0] + _wire_order(nseq)], *extra)


def _wire_order(size):
    ks = list(range(2, size))
    last = [k for k in ks if k % 2]
    return [k for k in ks if k % 2 == 0][::-1] + last[::-1] + [1]


def _swap(parts, axis, size, differences):
    got = dict([(0, parts[0])])
    for k in differences:
        got[k] = lax.ppermute(parts[k], axis, [(s, s ^ k) for s in range(size)])
    return got


def _halve(kept, sent, axis, size):
    step = 1
    while True:
        got = lax.ppermute(sent, axis, [(z, z ^ step) for z in range(size)])
        kept = kept + got.astype(F32)
        step *= 2
        if step == size:
            return kept[0]
        kept, sent = kept[0::2], kept[1::2].astype(BF16)


def _behind(parts, ahead, count):
    first = _wire_order(len(ahead))[:count]
    parts, arrived = lax.optimization_barrier((parts, [ahead[k] for k in first]))
    for k, part in zip(first, arrived):
        ahead[k] = part
    return parts


def _exchange(parts, axis):
    return lax.all_to_all(parts, axis, split_axis=0, concat_axis=0, tiled=True)


def _total(parts):
    return jnp.sum(parts.astype(F32), axis=0)


def local(tokens, gate, cotangent, first_factor, second_factor):
    seqs, _, width = tokens.shape
    ndp, nseq = lax.axis_size("dp"), lax.axis_size("seq")
    lb = first_factor.shape[0]
    lo, nb = second_factor.shape[:2]
    groups = lo // G
    early = groups // 4 if groups >= 8 else groups // 2
    late = early
    factor = 1.0 / float(width * seqs * ndp) ** 0.5
    me = jnp.stack([lax.axis_index("seq"), lax.axis_index("dp")]).astype(jnp.int32)

    s2_early = second_factor[:early * G].reshape(early * G * nb, nb)
    still = jnp.zeros_like(me)
    back_a = hidden_grad(still, s2_early, gate, cotangent, (), 0, early, False, nseq, lb, nb)
    second_factor, back_a = lax.optimization_barrier((second_factor, back_a))
    s2 = second_factor.reshape(lo * nb, nb)
    grad_a = lax.all_to_all(back_a, "seq", split_axis=0, concat_axis=0, tiled=True)
    back_b = hidden_grad(
        me, s2, gate, cotangent, (back_a,), early, groups - early, True, nseq, lb, nb
    )
    spans = ((0, groups - late), (groups - late, late))
    hidden_b, hidden_c = hidden_forward(
        me, first_factor, tokens, (back_b[0],), spans, nseq, lo, 1024
    )
    back_b, grad_a, hidden_b = lax.optimization_barrier((back_b, grad_a, hidden_b))
    grad_b = _swap(back_b, "seq", nseq, _wire_order(nseq))
    wire = _wire_order(nseq)
    got_b = _swap(_behind(hidden_b, grad_b, nseq - 3), "seq", nseq, wire)
    got_c = _swap(_behind(hidden_c, got_b, 3), "seq", nseq, wire)
    input_grad, kept, sent = block_grads(
        me, first_factor, tokens, grad_a, grad_b, (), nseq, ndp, factor, 1024
    )
    sent = _behind(sent, got_b, 2)

    first_share = _halve(kept, sent, "dp", ndp)

    gate_grad, terms = mixed_stage(
        me, s2, gate, cotangent, got_b, (), (sent,), 0, groups - late, groups,
        nseq, ndp, lb, nb, factor
    )
    gate_grad, terms = mixed_stage(
        me, s2, gate, cotangent, got_c, (gate_grad, terms), (), groups - late, late, groups,
        nseq, ndp, lb, nb, factor
    )
    share = nb // ndp
    second_share = _total(_exchange(terms, "dp")).reshape(groups, terms.shape[2], -1, share, G)
    second_share = second_share.transpose(0, 4, 3, 2, 1).reshape(lo, share, nb)
    return (input_grad, gate_grad, first_share, second_share)


def solution(mesh):
    placed = (
        P("dp", "seq", None),
        P("dp", "seq", None),
        P("dp", "seq", None),
        P("seq", None, None),
        P("seq", None, None),
    )
    return jax.shard_map(
        local,
        mesh=mesh,
        in_specs=placed,
        out_specs=(
            P("dp", "seq", None),
            P("dp", "seq", None),
            P("seq", "dp", None),
            P("seq", "dp", None),
        ),
        check_vma=False,
    )
```

time: 340 us -> 233 us (0.69)
  local copies, waits for them, and re-layouts: 77.9 us -> 8.29 us
  Pallas kernels: 0 us -> 61.6 us
  matrix products: 59.2 us -> 0 us
  waiting for transfers between devices: 169 us -> 120 us
  starting transfers between devices: 10.7 us -> 27.9 us
  between operations: 14.1 us -> 0.84 us
  blocking collectives: 0 us -> 9.72 us
    ppermute x0 -> x23, waiting for transfers between devices: none -> 117 us  [the longest x21 117 us: _swap(): got[k] = lax.ppermute(parts[k], axis, [(s, s ^ k) for s in range(size)])]
    all_to_all x2 -> x1, waiting for transfers between devices: 115 us -> 2.81 us  [local(): lax.all_to_all(back_a, 'seq', split_axis=0, concat_axis=0, tiled=True)]
    pallas_call x0 -> x6, Pallas kernels: none -> 61.6 us  [the longest x2 18.6 us: mixed_stage(): _call(functools.partial(mixed_kernel, nseq, ndp, lb, nb, factor), (ng,),...]
    dot_general x6 -> x0, matrix products: 59.2 us -> none  [the longest x1 12.2 us: local(): jnp.einsum('nbic,nbjc->bij', hidden_grad, blocks, preferred_element_type=...]
    reduce_scatter x2 -> x0, waiting for transfers between devices: 53.8 us -> none  [the longest x1 53.8 us: local(): lax.psum_scatter(first_terms, 'dp', scatter_dimension=1, tiled=True)]
    all_to_all x3 -> x0, local copies, waits for them, and re-layouts: 31.8 us -> none  [the longest x2 23.5 us: local(): lax.all_to_all(hidden, 'seq', split_axis=2, concat_axis=1, tiled=True)]
    convert_element_type x2 -> x0, local copies, waits for them, and re-layouts: 26.3 us -> none  [the longest x1 14.9 us: local(): hidden = jnp.einsum('bij,nbjc->nbic', first_factor, blocks, preferred_ele...]
    ppermute x0 -> x23, starting transfers between devices: none -> 22.6 us  [the longest x21 18.4 us: _swap(): got[k] = lax.ppermute(parts[k], axis, [(s, s ^ k) for s in range(size)])]
  transfers between devices with their start and end apart: 4 -> 24, of which waited for: 3 -> 11; matrix products, arithmetic and copies ran while one was open for 34% -> 3% of each run, Pallas kernels for 0% -> 25%
where the time goes in v1:
time: 233 us
  waiting for transfers between devices  120 us (52%)
  Pallas kernels  61.6 us (26%)
  starting transfers between devices  27.9 us (12%)
  blocking collectives  9.72 us (4%)
  local copies, waits for them, and re-layouts  8.29 us (4%)
  other arithmetic  4.79 us (2%)
    ppermute x21, waiting for transfers between devices, _swap(): got[k] = lax.ppermute(parts[k], axis, [(s, s ^ k) for s in range(size)])  117 us
    pallas_call x2, Pallas kernels, mixed_stage(): _call(functools.partial(mixed_kernel, nseq, ndp, lb, nb, factor), (ng,),...  18.6 us
    ppermute x21, starting transfers between devices, _swap(): got[k] = lax.ppermute(parts[k], axis, [(s, s ^ k) for s in range(size)])  18.4 us
    pallas_call x1, Pallas kernels, block_grads(): _call(functools.partial(block_grads_kernel, nseq, ndp, lo, factor), (lb /...  16.8 us
    pallas_call x2, Pallas kernels, hidden_grad(): _call(functools.partial(hidden_grad_kernel, nseq, lb, nb, split), (ng,),...  14.8 us
    pallas_call x1, Pallas kernels, hidden_forward(): _call(functools.partial(hidden_kernel, nseq, lo, spans), (lb // 2, width...  11.4 us
    all_to_all x1, blocking collectives, _exchange(): return lax.all_to_all(parts, axis, split_axis=0, concat_axis=0, tiled=True)  9.72 us
    all_to_all x1, starting transfers between devices, local(): lax.all_to_all(back_a, 'seq', split_axis=0, concat_axis=0, tiled=True)  5.32 us
  transfers between devices with their start and end apart: 24, of which 11 were waited for; matrix products, arithmetic and copies ran while one was open for 3% of the time, Pallas kernels for 25%

profile of v1, /device:TPU:0, one launch (start us, length us, event | category | flops | bytes accessed | tf_op | source)
XLA Modules:
  0.0 232.8 jit_solution(9976122157053582968)
XLA Ops:
  0.6 1.8 copy.17
  2.5 0.5 broadcast_1_me_ref.2.me_ref
  3.0 4.4 %hidden_grad.2.rest_0_ = bf16[8,2,2,16,2048]{4,3,2,1,0:T(8,128)(2,1)} custom-call(s32[2]{0:T(128)} %broadcast_1_me_ref.2.me_ref, bf16[512,32]{1,0:T(8,128)(2,1)} %bitcast.15, bf16[1,2048,2048]{2,1,0:T(8,128)(2,1)} %gate_ref.7, bf16[1,2048,2048]{2,1,0:T(8,128)(2,1)} %cot_ref.7), custom_call_target="tpu_custom_call" | custom-call | flops 536870912 | bytes 6291456 | tf_op jit(solution)/shard_map/hidden_grad/pallas_call | solution.py:85
  7.4 5.3 %all-to-all-start = ((bf16[8,2,2,16,2048]{4,3,2,1,0:T(8,128)(2,1)}), bf16[8,2,2,16,2048]{4,3,2,1,0:T(8,128)(2,1)S(1)}, u32[]{:S(2)}, u32[]{:S(2)}) async-start(bf16[8,2,2,16,2048]{4,3,2,1,0:T(8,128)(2,1)} %hidden_grad.2.rest_0_), calls=%async_computation | async-start | bytes 4194304 | tf_op jit(solution)/shard_map/all_to_all | solution.py:352
  12.8 1.5 copy.18
  14.3 0.6 pad_add_fusion.me_ref
  14.8 10.4 %hidden_grad.3 = (bf16[2,6,16,2048]{3,2,1,0:T(8,128)(2,1)}, bf16[2,6,16,2048]{3,2,1,0:T(8,128)(2,1)}, bf16[2,6,16,2048]{3,2,1,0:T(8,128)(2,1)}, bf16[2,6,16,2048...) custom-call(s32[2]{0:T(128)} %pad_add_fusion.me_ref, ...), custom_call_target="tpu_custom_call" | custom-call | flops 1610612736 | bytes 18874368 | tf_op jit(solution)/shard_map/hidden_grad/pallas_call | solution.py:85
  25.2 11.4 %hidden.1 = (bf16[2,6,16,2048]{3,2,1,0:T(8,128)(2,1)}, bf16[2,6,16,2048]{3,2,1,0:T(8,128)(2,1)}, bf16[2,6,16,2048]{3,2,1,0:T(8,128)(2,1)}, bf16[2,6,16,2048]{3,2...) custom-call(s32[2]{0:T(128)} %pad_add_fusion.me_ref, ...), custom_call_target="tpu_custom_call" | custom-call | flops 4294967296 | bytes 16777216 | tf_op jit(solution)/shard_map/hidden/pallas_call | solution.py:133
  36.6 2.8 %all-to-all-done.hg_ref = bf16[8,2,2,16,2048]{4,3,2,1,0:T(8,128)(2,1)S(1)} async-done(((bf16[8,2,2,16,2048]{4,3,2,1,0:T(8,128)(2,1)}), bf16[8,2,2,16,2048]{4,3,2,1,0:T(8,128)(2,1)S(1)}, u32[]{:S(2)}, u32[]{:S(2)}) %all-to-all-start) | async-done | bytes 2097184 | tf_op jit(solution)/shard_map/all_to_all | solution.py:352
  39.4 0.6 collective-permute-start
  40.0 1.4 collective-permute-start.1
  41.4 1.5 collective-permute-start.2
  42.9 1.7 collective-permute-start.4
  44.6 16.4 %collective-permute-done.rest_1_ = bf16[2,6,16,2048]{3,2,1,0:T(8,128)(2,1)S(1)} collective-permute-done((bf16[2,6,16,2048]{3,2,1,0:T(8,128)(2,1)}, bf16[2,6,16,2048]{3,2,1,0:T(8,128)(2,1)S(1)}, u32[]{:S(2)}, u32[]{:S(2)}) %collective-permute-start) | collective-permute-done | bytes 786464 | tf_op jit(solution)/shard_map/ppermute | solution.py:305
  61.0 16.9 %collective-permute-done.1.rest_2_ = bf16[2,6,16,2048]{3,2,1,0:T(8,128)(2,1)S(1)} collective-permute-done((bf16[2,6,16,2048]{3,2,1,0:T(8,128)(2,1)}, bf16[2,6,16,2048]{3,2,1,0:T(8,128)(2,1)S(1)}, u32[]{:S(2)}, u32[]{:S(2)}) %collective-permute-start.1) | collective-permute-done | bytes 786464 | tf_op jit(solution)/shard_map/ppermute | solution.py:305
  77.9 14.1 %collective-permute-done.3.rest_4_ = bf16[2,6,16,2048]{3,2,1,0:T(8,128)(2,1)S(1)} collective-permute-done((bf16[2,6,16,2048]{3,2,1,0:T(8,128)(2,1)}, bf16[2,6,16,2048]{3,2,1,0:T(8,128)(2,1)S(1)}, u32[]{:S(2)}, u32[]{:S(2)}) %collective-permute-start.3) | collective-permute-done | bytes 786464 | tf_op jit(solution)/shard_map/ppermute | solution.py:305
  92.0 16.2 %collective-permute-done.4.rest_5_ = bf16[2,6,16,2048]{3,2,1,0:T(8,128)(2,1)S(1)} collective-permute-done((bf16[2,6,16,2048]{3,2,1,0:T(8,128)(2,1)S(1)}, bf16[2,6,16,2048]{3,2,1,0:T(8,128)(2,1)S(1)}, u32[]{:S(2)}, u32[]{:S(2)}) %collective-permute-start.4) | collective-permute-done | bytes 786464 | tf_op jit(solution)/shard_map/ppermute | solution.py:305
  108.2 1.0 collective-permute-start.7
  109.2 1.5 collective-permute-start.8
  110.7 1.0 collective-permute-start.9
  111.7 0.9 copy-done.18
  112.6 16.8 %block_grads.1 = (bf16[1,2048,2048]{2,1,0:T(8,128)(2,1)}, f32[2,4,128,512]{3,2,1,0:T(8,128)}, bf16[2,4,128,512]{3,2,1,0:T(8,128)(2,1)}) custom-call(s32[2]{0:T(128)} %pad_add_fusion.me_ref, bf16[4,512,512]{2,1,0:T(8,128)(2,1)} %f_ref.3, bf16[1,2048,2048]{2,1,0:T(8,128)(2,1)} %x_ref.3, bf16[8,2,2,16,2048]{4,3,2,1,0:T(8,128)(2,1)} %copy-done, ...), custom_call_target="tpu_custom_call" | custom-call | flops 8589934592 | bytes 25165824 | tf_op jit(solution)/shard_map/block_grads/pallas_call | solution.py:197
  129.5 0.3 collective-permute-done.7.rest_1_
  129.7 16.1 %collective-permute-done.8.rest_2_ = bf16[2,6,16,2048]{3,2,1,0:T(8,128)(2,1)} collective-permute-done((bf16[2,6,16,2048]{3,2,1,0:T(8,128)(2,1)}, bf16[2,6,16,2048]{3,2,1,0:T(8,128)(2,1)}, u32[]{:S(2)}, u32[]{:S(2)}) %collective-permute-start.8) | collective-permute-done | bytes 786464 | tf_op jit(solution)/shard_map/ppermute | solution.py:305
  145.8 0.3 collective-permute-done.9.rest_3_
  146.1 1.6 collective-permute-start.21
  147.7 0.8 collective-permute-start.17
  148.5 1.9 collective-permute-start.18
  150.4 0.6 collective-permute-start.20
  151.0 17.7 %collective-permute-done.17.rest_4_ = bf16[2,6,16,2048]{3,2,1,0:T(8,128)(2,1)S(1)} collective-permute-done((bf16[2,6,16,2048]{3,2,1,0:T(8,128)(2,1)}, bf16[2,6,16,2048]{3,2,1,0:T(8,128)(2,1)S(1)}, u32[]{:S(2)}, u32[]{:S(2)}) %collective-permute-start.17) | collective-permute-done | bytes 786464 | tf_op jit(solution)/shard_map/ppermute | solution.py:305
  168.7 1.6 collective-permute-start.10
  170.2 15.0 %collective-permute-done.18.rest_5_ = bf16[2,6,16,2048]{3,2,1,0:T(8,128)(2,1)S(1)} collective-permute-done((bf16[2,6,16,2048]{3,2,1,0:T(8,128)(2,1)}, bf16[2,6,16,2048]{3,2,1,0:T(8,128)(2,1)S(1)}, u32[]{:S(2)}, u32[]{:S(2)}) %collective-permute-start.18) | collective-permute-done | bytes 786464 | tf_op jit(solution)/shard_map/ppermute | solution.py:305
  185.2 1.5 collective-permute-start.11
  186.8 0.6 collective-permute-start.12
  187.4 2.0 convert_add_fusion
  189.4 0.9 slice.21
  190.2 0.8 collective-permute-start.13
  191.1 1.8 collective-permute-start.14
  192.9 3.8 %collective-permute-done.11.rest_2_ = bf16[2,2,16,2048]{3,2,1,0:T(8,128)(2,1)S(1)} collective-permute-done((bf16[2,2,16,2048]{3,2,1,0:T(8,128)(2,1)S(1)}, bf16[2,2,16,2048]{3,2,1,0:T(8,128)(2,1)S(1)}, u32[]{:S(2)}, u32[]{:S(2)}) %collective-permute-start.11) | collective-permute-done | bytes 262176 | tf_op jit(solution)/shard_map/ppermute | solution.py:305
  196.8 2.6 %collective-permute-start.22 = (bf16[1,4,128,512]{3,2,1,0:T(8,128)(2,1)}, bf16[1,4,128,512]{3,2,1,0:T(8,128)(2,1)}, u32[]{:S(2)}, u32[]{:S(2)}) collective-permute-start(bf16[1,4,128,512]{3,2,1,0:T(8,128)(2,1)} %slice.21), channel_id=1, source_target_pairs={{0,16},{8,24},{16,0},{24,8},{1,17},{9,25},{17,1},{25,9},{2,18},{10... | collective-permute-start | bytes 1572872 | tf_op jit(solution)/shard_map/ppermute | solution.py:312
  199.4 12.7 %mixed.2 = (bf16[1,2048,2048]{2,1,0:T(8,128)(2,1)}, bf16[4,8,16,128]{3,2,1,0:T(8,128)(2,1)}) custom-call(s32[2]{0:T(128)} %pad_add_fusion.me_ref, bf16[2048,32]{1,0:T(8,128)(2,1)} %bitcast.11, bf16[1,2048,2048]{2,1,0:T(8,128)(2,1)} %gate_ref.7, bf16[1,2048,2048]{2,1,0:T(8,128)(2,1)} %cot_ref.7, bf16[2,6,16,2048]{3,2,1,0:T(8,128)(2,1)} %get-tuple-element.141.rest_0_, ...), custom_call_target="tpu_custom_call" | custom-call | flops 3221225472 | bytes 25165824 | tf_op jit(solution)/shard_map/mixed/pallas_call | solution.py:269
  212.3 0.6 copy-done.8
  213.2 5.9 %mixed.3 = (bf16[1,2048,2048]{2,1,0:T(8,128)(2,1)}, bf16[4,8,16,128]{3,2,1,0:T(8,128)(2,1)}) custom-call(s32[2]{0:T(128)} %pad_add_fusion.me_ref, bf16[2048,32]{1,0:T(8,128)(2,1)} %bitcast.12, bf16[1,2048,2048]{2,1,0:T(8,128)(2,1)} %gate_ref.7, bf16[1,2048,2048]{2,1,0:T(8,128)(2,1)} %cot_ref.7, ...), custom_call_target="tpu_custom_call", output_to_operand_aliasing={{0}: (12, {}), {1}: (13, {})} | custom-call | flops 1073741824 | bytes 8388608 | tf_op jit(solution)/shard_map/mixed/pallas_call | solution.py:269
  219.1 9.7 %all_to_all.10 = bf16[4,8,16,128]{3,2,1,0:T(8,128)(2,1)S(1)} all-to-all(bf16[4,8,16,128]{3,2,1,0:T(8,128)(2,1)} %get-tuple-element.157), channel_id=1, replica_groups=mesh['dp'=4,'seq'=8] {'dp'}, dimensions={0} | all-to-all | bytes 262144 | tf_op jit(solution)/shard_map/all_to_all | solution.py:329
  229.0 0.4 copy.20
  229.4 0.3 reshape.23
  229.7 0.8 copy.21
  230.6 2.2 fusion
  (59 shorter events, 0.7 us)
Async XLA Ops:
  7.4 5.3 %copy-start.1 = (bf16[64,32,32]{0,2,1:T(8,128)(2,1)S(1)}, bf16[64,32,32]{0,2,1:T(8,128)(2,1)}, u32[]{:S(2)}) copy-start(bf16[64,32,32]{0,2,1:T(8,128)(2,1)} %param.9) | copy-start | bytes 393220
  7.4 32.0 %all-to-all-start = ((bf16[8,2,2,16,2048]{4,3,2,1,0:T(8,128)(2,1)}), bf16[8,2,2,16,2048]{4,3,2,1,0:T(8,128)(2,1)S(1)}, u32[]{:S(2)}, u32[]{:S(2)}) async-start(bf16[8,2,2,16,2048]{4,3,2,1,0:T(8,128)(2,1)} %hidden_grad.2.rest_0_), calls=%async_computation | async-start | bytes 4194304 | tf_op jit(solution)/shard_map/all_to_all | solution.py:352
  25.2 17.7 %copy-start.12 = (bf16[2,6,16,2048]{3,2,1,0:T(8,128)(2,1)S(1)}, bf16[2,6,16,2048]{3,2,1,0:T(8,128)(2,1)}, u32[]{:S(2)}) copy-start(bf16[2,6,16,2048]{3,2,1,0:T(8,128)(2,1)} %get-tuple-element.113) | copy-start | bytes 2359300
  39.4 73.2 %copy-start = (bf16[8,2,2,16,2048]{4,3,2,1,0:T(8,128)(2,1)}, bf16[8,2,2,16,2048]{4,3,2,1,0:T(8,128)(2,1)S(1)}, u32[]{:S(2)}) copy-start(bf16[8,2,2,16,2048]{4,3,2,1,0:T(8,128)(2,1)S(1)} %all-to-all-done.hg_ref) | copy-start | bytes 6291460
  39.4 145.9 %copy-start.19 = (bf16[2,2,16,2048]{3,2,1,0:T(8,128)(2,1)S(1)}, bf16[2,2,16,2048]{3,2,1,0:T(8,128)(2,1)}, u32[]{:S(2)}) copy-start(bf16[2,2,16,2048]{3,2,1,0:T(8,128)(2,1)} %get-tuple-element.135) | copy-start | bytes 786436
  39.4 21.6 %collective-permute-start = (bf16[2,6,16,2048]{3,2,1,0:T(8,128)(2,1)}, bf16[2,6,16,2048]{3,2,1,0:T(8,128)(2,1)S(1)}, u32[]{:S(2)}, u32[]{:S(2)}) collective-permute-start(bf16[2,6,16,2048]{3,2,1,0:T(8,128)(2,1)} %get-tuple-element.109), channel_id=1, source_target_pairs={{0,6},{1,7},{2,4},{3,5},{4,2},{5,3},{6,0},{7,1},{8,14},{9,15},{10,... | collective-permute-start | bytes 2359304 | tf_op jit(solution)/shard_map/ppermute | solution.py:305
  40.0 37.9 %collective-permute-start.1 = (bf16[2,6,16,2048]{3,2,1,0:T(8,128)(2,1)}, bf16[2,6,16,2048]{3,2,1,0:T(8,128)(2,1)S(1)}, u32[]{:S(2)}, u32[]{:S(2)}) collective-permute-start(bf16[2,6,16,2048]{3,2,1,0:T(8,128)(2,1)} %get-tuple-element.110), channel_id=1, source_target_pairs={{0,4},{1,5},{2,6},{3,7},{4,0},{5,1},{6,2},{7,3},{8,12},{9,13},{10,... | collective-permute-start | bytes 2359304 | tf_op jit(solution)/shard_map/ppermute | solution.py:305
  41.4 36.6 %collective-permute-start.2 = (bf16[2,6,16,2048]{3,2,1,0:T(8,128)(2,1)}, bf16[2,6,16,2048]{3,2,1,0:T(8,128)(2,1)S(1)}, u32[]{:S(2)}, u32[]{:S(2)}) collective-permute-start(bf16[2,6,16,2048]{3,2,1,0:T(8,128)(2,1)} %get-tuple-element.111), channel_id=1, source_target_pairs={{0,2},{1,3},{2,0},{3,1},{4,6},{5,7},{6,4},{7,5},{8,10},{9,11},{10,... | collective-permute-start | bytes 2359304 | tf_op jit(solution)/shard_map/ppermute | solution.py:305
  42.9 49.1 %collective-permute-start.3 = (bf16[2,6,16,2048]{3,2,1,0:T(8,128)(2,1)}, bf16[2,6,16,2048]{3,2,1,0:T(8,128)(2,1)S(1)}, u32[]{:S(2)}, u32[]{:S(2)}) collective-permute-start(bf16[2,6,16,2048]{3,2,1,0:T(8,128)(2,1)} %get-tuple-element.112), channel_id=1, source_target_pairs={{0,7},{1,6},{2,5},{3,4},{4,3},{5,2},{6,1},{7,0},{8,15},{9,14},{10,... | collective-permute-start | bytes 2359304 | tf_op jit(solution)/shard_map/ppermute | solution.py:305
  42.9 65.3 %collective-permute-start.4 = (bf16[2,6,16,2048]{3,2,1,0:T(8,128)(2,1)S(1)}, bf16[2,6,16,2048]{3,2,1,0:T(8,128)(2,1)S(1)}, u32[]{:S(2)}, u32[]{:S(2)}) collective-permute-start(bf16[2,6,16,2048]{3,2,1,0:T(8,128)(2,1)S(1)} %copy-done.12), channel_id=1, source_target_pairs={{0,5},{1,4},{2,7},{3,6},{4,1},{5,0},{6,3},{7,2},{8,13},{9,12},{10,... | collective-permute-start | bytes 2359304 | tf_op jit(solution)/shard_map/ppermute | solution.py:305
  61.0 47.2 %copy-start.13 = (bf16[2,6,16,2048]{3,2,1,0:T(8,128)(2,1)}, bf16[2,6,16,2048]{3,2,1,0:T(8,128)(2,1)S(1)}, u32[]{:S(2)}) copy-start(bf16[2,6,16,2048]{3,2,1,0:T(8,128)(2,1)S(1)} %collective-permute-done.rest_1_) | copy-start | bytes 2359300
  61.0 50.7 %collective-permute-start.5 = (bf16[2,6,16,2048]{3,2,1,0:T(8,128)(2,1)}, bf16[2,6,16,2048]{3,2,1,0:T(8,128)(2,1)S(1)}, u32[]{:S(2)}, u32[]{:S(2)}) collective-permute-start(bf16[2,6,16,2048]{3,2,1,0:T(8,128)(2,1)} %get-tuple-element.119), channel_id=1, source_target_pairs={{0,3},{1,2},{2,1},{3,0},{4,7},{5,6},{6,5},{7,4},{8,11},{9,10},{10,... | collective-permute-start | bytes 2359304 | tf_op jit(solution)/shard_map/ppermute | solution.py:305
  77.9 31.3 %copy-start.14 = (bf16[2,6,16,2048]{3,2,1,0:T(8,128)(2,1)}, bf16[2,6,16,2048]{3,2,1,0:T(8,128)(2,1)S(1)}, u32[]{:S(2)}) copy-start(bf16[2,6,16,2048]{3,2,1,0:T(8,128)(2,1)S(1)} %collective-permute-done.1.rest_2_) | copy-start | bytes 2359300
  77.9 34.7 %collective-permute-start.6 = (bf16[2,6,16,2048]{3,2,1,0:T(8,128)(2,1)}, bf16[2,6,16,2048]{3,2,1,0:T(8,128)(2,1)}, u32[]{:S(2)}, u32[]{:S(2)}) collective-permute-start(bf16[2,6,16,2048]{3,2,1,0:T(8,128)(2,1)} %get-tuple-element.120), channel_id=1, source_target_pairs={{0,1},{1,0},{2,3},{3,2},{4,5},{5,4},{6,7},{7,6},{8,9},{9,8},{10,11... | collective-permute-start | bytes 2359304 | tf_op jit(solution)/shard_map/ppermute | solution.py:305
  77.9 32.8 %copy-start.15 = (bf16[2,6,16,2048]{3,2,1,0:T(8,128)(2,1)}, bf16[2,6,16,2048]{3,2,1,0:T(8,128)(2,1)S(1)}, u32[]{:S(2)}) copy-start(bf16[2,6,16,2048]{3,2,1,0:T(8,128)(2,1)S(1)} %collective-permute-done.2.rest_3_) | copy-start | bytes 2359300
  92.0 19.7 %copy-start.16 = (bf16[2,6,16,2048]{3,2,1,0:T(8,128)(2,1)}, bf16[2,6,16,2048]{3,2,1,0:T(8,128)(2,1)S(1)}, u32[]{:S(2)}) copy-start(bf16[2,6,16,2048]{3,2,1,0:T(8,128)(2,1)S(1)} %collective-permute-done.3.rest_4_) | copy-start | bytes 2359300
  108.2 3.5 %copy-start.17 = (bf16[2,6,16,2048]{3,2,1,0:T(8,128)(2,1)}, bf16[2,6,16,2048]{3,2,1,0:T(8,128)(2,1)S(1)}, u32[]{:S(2)}) copy-start(bf16[2,6,16,2048]{3,2,1,0:T(8,128)(2,1)S(1)} %collective-permute-done.4.rest_5_) | copy-start | bytes 2359300
  108.2 21.5 %collective-permute-start.7 = (bf16[2,6,16,2048]{3,2,1,0:T(8,128)(2,1)}, bf16[2,6,16,2048]{3,2,1,0:T(8,128)(2,1)S(1)}, u32[]{:S(2)}, u32[]{:S(2)}) collective-permute-start(bf16[2,6,16,2048]{3,2,1,0:T(8,128)(2,1)} %get-tuple-element.130), channel_id=1, source_target_pairs={{0,6},{1,7},{2,4},{3,5},{4,2},{5,3},{6,0},{7,1},{8,14},{9,15},{10,... | collective-permute-start | bytes 2359304 | tf_op jit(solution)/shard_map/ppermute | solution.py:305
  109.2 36.6 %collective-permute-start.8 = (bf16[2,6,16,2048]{3,2,1,0:T(8,128)(2,1)}, bf16[2,6,16,2048]{3,2,1,0:T(8,128)(2,1)}, u32[]{:S(2)}, u32[]{:S(2)}) collective-permute-start(bf16[2,6,16,2048]{3,2,1,0:T(8,128)(2,1)} %get-tuple-element.131), channel_id=1, source_target_pairs={{0,4},{1,5},{2,6},{3,7},{4,0},{5,1},{6,2},{7,3},{8,12},{9,13},{10,... | collective-permute-start | bytes 2359304 | tf_op jit(solution)/shard_map/ppermute | solution.py:305
  110.7 35.4 %collective-permute-start.9 = (bf16[2,6,16,2048]{3,2,1,0:T(8,128)(2,1)}, bf16[2,6,16,2048]{3,2,1,0:T(8,128)(2,1)}, u32[]{:S(2)}, u32[]{:S(2)}) collective-permute-start(bf16[2,6,16,2048]{3,2,1,0:T(8,128)(2,1)} %get-tuple-element.132), channel_id=1, source_target_pairs={{0,2},{1,3},{2,0},{3,1},{4,6},{5,7},{6,4},{7,5},{8,10},{9,11},{10,... | collective-permute-start | bytes 2359304 | tf_op jit(solution)/shard_map/ppermute | solution.py:305
  111.7 0.9 copy-start.18
  129.7 59.6 %copy-start.2 = (bf16[2,6,16,2048]{3,2,1,0:T(8,128)(2,1)}, bf16[2,6,16,2048]{3,2,1,0:T(8,128)(2,1)S(1)}, u32[]{:S(2)}) copy-start(bf16[2,6,16,2048]{3,2,1,0:T(8,128)(2,1)S(1)} %collective-permute-done.7.rest_1_) | copy-start | bytes 2359300
  146.1 40.7 %collective-permute-start.21 = (bf16[2,4,128,512]{3,2,1,0:T(8,128)(2,1)}, bf16[2,4,128,512]{3,2,1,0:T(8,128)(2,1)S(1)}, u32[]{:S(2)}, u32[]{:S(2)}) collective-permute-start(bf16[2,4,128,512]{3,2,1,0:T(8,128)(2,1)} %get-tuple-element.152.rest_8_), channel_id=1, source_target_pairs={{0,8},{8,0},{16,24},{24,16},{1,9},{9,1},{17,25},{25,17},{2,10},{10... | collective-permute-start | bytes 3145736 | tf_op jit(solution)/shard_map/ppermute | solution.py:312
  147.7 21.0 %collective-permute-start.17 = (bf16[2,6,16,2048]{3,2,1,0:T(8,128)(2,1)}, bf16[2,6,16,2048]{3,2,1,0:T(8,128)(2,1)S(1)}, u32[]{:S(2)}, u32[]{:S(2)}) collective-permute-start(bf16[2,6,16,2048]{3,2,1,0:T(8,128)(2,1)} %get-tuple-element.148), channel_id=1, source_target_pairs={{0,7},{1,6},{2,5},{3,4},{4,3},{5,2},{6,1},{7,0},{8,15},{9,14},{10,... | collective-permute-start | bytes 2359304 | tf_op jit(solution)/shard_map/ppermute | solution.py:305
  148.5 36.8 %collective-permute-start.18 = (bf16[2,6,16,2048]{3,2,1,0:T(8,128)(2,1)}, bf16[2,6,16,2048]{3,2,1,0:T(8,128)(2,1)S(1)}, u32[]{:S(2)}, u32[]{:S(2)}) collective-permute-start(bf16[2,6,16,2048]{3,2,1,0:T(8,128)(2,1)} %get-tuple-element.149), channel_id=1, source_target_pairs={{0,5},{1,4},{2,7},{3,6},{4,1},{5,0},{6,3},{7,2},{8,13},{9,12},{10,... | collective-permute-start | bytes 2359304 | tf_op jit(solution)/shard_map/ppermute | solution.py:305
  150.4 39.9 %collective-permute-start.19 = (bf16[2,6,16,2048]{3,2,1,0:T(8,128)(2,1)}, bf16[2,6,16,2048]{3,2,1,0:T(8,128)(2,1)}, u32[]{:S(2)}, u32[]{:S(2)}) collective-permute-start(bf16[2,6,16,2048]{3,2,1,0:T(8,128)(2,1)} %get-tuple-element.150), channel_id=1, source_target_pairs={{0,3},{1,2},{2,1},{3,0},{4,7},{5,6},{6,5},{7,4},{8,11},{9,10},{10,... | collective-permute-start | bytes 2359304 | tf_op jit(solution)/shard_map/ppermute | solution.py:305
  150.4 40.7 %collective-permute-start.20 = (bf16[2,6,16,2048]{3,2,1,0:T(8,128)(2,1)}, bf16[2,6,16,2048]{3,2,1,0:T(8,128)(2,1)}, u32[]{:S(2)}, u32[]{:S(2)}) collective-permute-start(bf16[2,6,16,2048]{3,2,1,0:T(8,128)(2,1)} %get-tuple-element.151), channel_id=1, source_target_pairs={{0,1},{1,0},{2,3},{3,2},{4,5},{5,4},{6,7},{7,6},{8,9},{9,8},{10,11... | collective-permute-start | bytes 2359304 | tf_op jit(solution)/shard_map/ppermute | solution.py:305
  168.7 18.7 %copy-start.3 = (bf16[2,6,16,2048]{3,2,1,0:T(8,128)(2,1)}, bf16[2,6,16,2048]{3,2,1,0:T(8,128)(2,1)S(1)}, u32[]{:S(2)}) copy-start(bf16[2,6,16,2048]{3,2,1,0:T(8,128)(2,1)S(1)} %collective-permute-done.17.rest_4_) | copy-start | bytes 2359300
  168.7 24.2 %collective-permute-start.10 = (bf16[2,2,16,2048]{3,2,1,0:T(8,128)(2,1)}, bf16[2,2,16,2048]{3,2,1,0:T(8,128)(2,1)S(1)}, u32[]{:S(2)}, u32[]{:S(2)}) collective-permute-start(bf16[2,2,16,2048]{3,2,1,0:T(8,128)(2,1)} %get-tuple-element.134), channel_id=1, source_target_pairs={{0,6},{1,7},{2,4},{3,5},{4,2},{5,3},{6,0},{7,1},{8,14},{9,15},{10,... | collective-permute-start | bytes 786440 | tf_op jit(solution)/shard_map/ppermute | solution.py:305
  185.2 2.1 copy-start.4
  185.2 11.5 %collective-permute-start.11 = (bf16[2,2,16,2048]{3,2,1,0:T(8,128)(2,1)S(1)}, bf16[2,2,16,2048]{3,2,1,0:T(8,128)(2,1)S(1)}, u32[]{:S(2)}, u32[]{:S(2)}) collective-permute-start(bf16[2,2,16,2048]{3,2,1,0:T(8,128)(2,1)S(1)} %copy-done.19), channel_id=1, source_target_pairs={{0,4},{1,5},{2,6},{3,7},{4,0},{5,1},{6,2},{7,3},{8,12},{9,13},{10,... | collective-permute-start | bytes 786440 | tf_op jit(solution)/shard_map/ppermute | solution.py:305
  186.8 10.0 %collective-permute-start.12 = (bf16[2,2,16,2048]{3,2,1,0:T(8,128)(2,1)}, bf16[2,2,16,2048]{3,2,1,0:T(8,128)(2,1)S(1)}, u32[]{:S(2)}, u32[]{:S(2)}) collective-permute-start(bf16[2,2,16,2048]{3,2,1,0:T(8,128)(2,1)} %get-tuple-element.136), channel_id=1, source_target_pairs={{0,2},{1,3},{2,0},{3,1},{4,6},{5,7},{6,4},{7,5},{8,10},{9,11},{10,... | collective-permute-start | bytes 786440 | tf_op jit(solution)/shard_map/ppermute | solution.py:305
  190.2 22.0 %collective-permute-start.13 = (bf16[2,2,16,2048]{3,2,1,0:T(8,128)(2,1)}, bf16[2,2,16,2048]{3,2,1,0:T(8,128)(2,1)S(1)}, u32[]{:S(2)}, u32[]{:S(2)}) collective-permute-start(bf16[2,2,16,2048]{3,2,1,0:T(8,128)(2,1)} %get-tuple-element.137), channel_id=1, source_target_pairs={{0,7},{1,6},{2,5},{3,4},{4,3},{5,2},{6,1},{7,0},{8,15},{9,14},{10,... | collective-permute-start | bytes 786440 | tf_op jit(solution)/shard_map/ppermute | solution.py:305
  191.1 21.1 %collective-permute-start.14 = (bf16[2,2,16,2048]{3,2,1,0:T(8,128)(2,1)}, bf16[2,2,16,2048]{3,2,1,0:T(8,128)(2,1)S(1)}, u32[]{:S(2)}, u32[]{:S(2)}) collective-permute-start(bf16[2,2,16,2048]{3,2,1,0:T(8,128)(2,1)} %get-tuple-element.138), channel_id=1, source_target_pairs={{0,5},{1,4},{2,7},{3,6},{4,1},{5,0},{6,3},{7,2},{8,13},{9,12},{10,... | collective-permute-start | bytes 786440 | tf_op jit(solution)/shard_map/ppermute | solution.py:305
  192.9 19.3 %copy-start.5 = (bf16[2,2,16,2048]{3,2,1,0:T(8,128)(2,1)}, bf16[2,2,16,2048]{3,2,1,0:T(8,128)(2,1)S(1)}, u32[]{:S(2)}) copy-start(bf16[2,2,16,2048]{3,2,1,0:T(8,128)(2,1)S(1)} %collective-permute-done.10.rest_1_) | copy-start | bytes 786436
  192.9 19.4 %collective-permute-start.15 = (bf16[2,2,16,2048]{3,2,1,0:T(8,128)(2,1)}, bf16[2,2,16,2048]{3,2,1,0:T(8,128)(2,1)S(1)}, u32[]{:S(2)}, u32[]{:S(2)}) collective-permute-start(bf16[2,2,16,2048]{3,2,1,0:T(8,128)(2,1)} %get-tuple-element.139), channel_id=1, source_target_pairs={{0,3},{1,2},{2,1},{3,0},{4,7},{5,6},{6,5},{7,4},{8,11},{9,10},{10,... | collective-permute-start | bytes 786440 | tf_op jit(solution)/shard_map/ppermute | solution.py:305
  196.8 15.4 %copy-start.6 = (bf16[2,2,16,2048]{3,2,1,0:T(8,128)(2,1)}, bf16[2,2,16,2048]{3,2,1,0:T(8,128)(2,1)S(1)}, u32[]{:S(2)}) copy-start(bf16[2,2,16,2048]{3,2,1,0:T(8,128)(2,1)S(1)} %collective-permute-done.11.rest_2_) | copy-start | bytes 786436
  196.8 15.5 %collective-permute-start.16 = (bf16[2,2,16,2048]{3,2,1,0:T(8,128)(2,1)}, bf16[2,2,16,2048]{3,2,1,0:T(8,128)(2,1)S(1)}, u32[]{:S(2)}, u32[]{:S(2)}) collective-permute-start(bf16[2,2,16,2048]{3,2,1,0:T(8,128)(2,1)} %get-tuple-element.140), channel_id=1, source_target_pairs={{0,1},{1,0},{2,3},{3,2},{4,5},{5,4},{6,7},{7,6},{8,9},{9,8},{10,11... | collective-permute-start | bytes 786440 | tf_op jit(solution)/shard_map/ppermute | solution.py:305
  196.8 15.4 %copy-start.7 = (bf16[2,2,16,2048]{3,2,1,0:T(8,128)(2,1)}, bf16[2,2,16,2048]{3,2,1,0:T(8,128)(2,1)S(1)}, u32[]{:S(2)}) copy-start(bf16[2,2,16,2048]{3,2,1,0:T(8,128)(2,1)S(1)} %collective-permute-done.12.rest_3_) | copy-start | bytes 786436
  196.8 33.7 %collective-permute-start.22 = (bf16[1,4,128,512]{3,2,1,0:T(8,128)(2,1)}, bf16[1,4,128,512]{3,2,1,0:T(8,128)(2,1)}, u32[]{:S(2)}, u32[]{:S(2)}) collective-permute-start(bf16[1,4,128,512]{3,2,1,0:T(8,128)(2,1)} %slice.21), channel_id=1, source_target_pairs={{0,16},{8,24},{16,0},{24,8},{1,17},{9,25},{17,1},{25,9},{2,18},{10... | collective-permute-start | bytes 1572872 | tf_op jit(solution)/shard_map/ppermute | solution.py:312
  212.2 0.7 copy-start.8
  212.2 0.8 copy-start.9
  212.3 0.8 copy-start.10
  212.3 0.9 copy-start.11

commit v2 on v1

--- a/solution.py
+++ b/solution.py
@@ -2,6 +2,7 @@
 
 import jax
 import jax.numpy as jnp
+import numpy as np
 from jax import lax
 from jax.experimental import pallas as pl
 from jax.experimental.pallas import tpu as pltpu
@@ -306,15 +307,18 @@
     return got
 
 
-def _halve(kept, sent, axis, size):
-    step = 1
-    while True:
-        got = lax.ppermute(sent, axis, [(z, z ^ step) for z in range(size)])
+def _pass(part, axis, size, step):
+    return lax.ppermute(part, axis, [(z, z ^ step) for z in range(size)])
+
+
+def _halve(kept, got, axis, size):
+    step = 2
+    while step < size:
         kept = kept + got.astype(F32)
+        got = _pass(kept[1::2].astype(BF16), axis, size, step)
+        kept = kept[0::2]
         step *= 2
-        if step == size:
-            return kept[0]
-        kept, sent = kept[0::2], kept[1::2].astype(BF16)
+    return kept, got
 
 
 def _behind(parts, ahead, count):
@@ -345,7 +349,7 @@
     me = jnp.stack([lax.axis_index("seq"), lax.axis_index("dp")]).astype(jnp.int32)
 
     s2_early = second_factor[:early * G].reshape(early * G * nb, nb)
-    still = jnp.zeros_like(me)
+    still = np.array([0, 1], np.int32)
     back_a = hidden_grad(still, s2_early, gate, cotangent, (), 0, early, False, nseq, lb, nb)
     second_factor, back_a = lax.optimization_barrier((second_factor, back_a))
     s2 = second_factor.reshape(lo * nb, nb)
@@ -361,23 +365,30 @@
     grad_b = _swap(back_b, "seq", nseq, _wire_order(nseq))
     wire = _wire_order(nseq)
     got_b = _swap(_behind(hidden_b, grad_b, nseq - 3), "seq", nseq, wire)
-    got_c = _swap(_behind(hidden_c, got_b, 3), "seq", nseq, wire)
+    hidden_c = _behind(hidden_c, got_b, 3)
+    got_c = _swap(hidden_c, "seq", nseq, wire[:-1])
     input_grad, kept, sent = block_grads(
         me, first_factor, tokens, grad_a, grad_b, (), nseq, ndp, factor, 1024
     )
     sent = _behind(sent, got_b, 2)
 
-    first_share = _halve(kept, sent, "dp", ndp)
+    halves = _pass(sent, "dp", ndp, 1)
 
     gate_grad, terms = mixed_stage(
         me, s2, gate, cotangent, got_b, (), (sent,), 0, groups - late, groups,
         nseq, ndp, lb, nb, factor
     )
+    last_c, terms = lax.optimization_barrier((hidden_c[wire[-1]], terms))
+    hidden_c[wire[-1]] = last_c
+    got_c.update(_swap(hidden_c, "seq", nseq, wire[-1:]))
+    kept, first_got = _halve(kept, halves, "dp", ndp)
     gate_grad, terms = mixed_stage(
         me, s2, gate, cotangent, got_c, (gate_grad, terms), (), groups - late, late, groups,
         nseq, ndp, lb, nb, factor
     )
     share = nb // ndp
+    terms, first_got = lax.optimization_barrier((terms, first_got))
+    first_share = (kept + first_got.astype(F32))[0]
     second_share = _total(_exchange(terms, "dp")).reshape(groups, terms.shape[2], -1, share, G)
     second_share = second_share.transpose(0, 4, 3, 2, 1).reshape(lo, share, nb)
     return (input_grad, gate_grad, first_share, second_share)

time: 233 us -> 230 us (0.987)
  blocking collectives: 9.72 us -> 0 us
  starting transfers between devices: 27.9 us -> 32.6 us
  waiting for transfers between devices: 120 us -> 124 us
    ppermute x21, waiting for transfers between devices: 117 us -> 95.9 us  [_swap(): got[k] = lax.ppermute(parts[k], axis, [(s, s ^ k) for s in range(size)])]
    ppermute x2, waiting for transfers between devices: 0.01 us -> 20.3 us  [_pass(): return lax.ppermute(part, axis, [(z, z ^ step) for z in range(size)])]
    all_to_all x1 -> x0, blocking collectives: 9.72 us -> none  [_exchange(): return lax.all_to_all(parts, axis, split_axis=0, concat_axis=0, tiled=True)]
    all_to_all x0 -> x1, waiting for transfers between devices: none -> 5.3 us  [_exchange(): return lax.all_to_all(parts, axis, split_axis=0, concat_axis=0, tiled=True)]
    all_to_all x0 -> x1, starting transfers between devices: none -> 3.34 us  [_exchange(): return lax.all_to_all(parts, axis, split_axis=0, concat_axis=0, tiled=True)]
  transfers between devices with their start and end apart: 24 -> 25, of which waited for: 11 -> 13; matrix products, arithmetic and copies ran while one was open for 3% -> 2% of each run, Pallas kernels for 25% -> 25%
where the time goes in v2:
time: 230 us
  waiting for transfers between devices  124 us (54%)
  Pallas kernels  61.6 us (27%)
  starting transfers between devices  32.6 us (14%)
  local copies, waits for them, and re-layouts  6.57 us (3%)
  other arithmetic  3.83 us (2%)
    ppermute x21, waiting for transfers between devices, _swap(): got[k] = lax.ppermute(parts[k], axis, [(s, s ^ k) for s in range(size)])  95.9 us
    ppermute x2, waiting for transfers between devices, _pass(): return lax.ppermute(part, axis, [(z, z ^ step) for z in range(size)])  20.3 us
    ppermute x21, starting transfers between devices, _swap(): got[k] = lax.ppermute(parts[k], axis, [(s, s ^ k) for s in range(size)])  19.8 us
    pallas_call x2, Pallas kernels, mixed_stage(): _call(functools.partial(mixed_kernel, nseq, ndp, lb, nb, factor), (ng,),...  18.6 us
    pallas_call x1, Pallas kernels, block_grads(): _call(functools.partial(block_grads_kernel, nseq, ndp, lo, factor), (lb /...  16.8 us
    pallas_call x2, Pallas kernels, hidden_grad(): _call(functools.partial(hidden_grad_kernel, nseq, lb, nb, split), (ng,),...  14.8 us
    pallas_call x1, Pallas kernels, hidden_forward(): _call(functools.partial(hidden_kernel, nseq, lo, spans), (lb // 2, width...  11.3 us
    all_to_all x1, starting transfers between devices, local(): lax.all_to_all(back_a, 'seq', split_axis=0, concat_axis=0, tiled=True)  5.32 us
  transfers between devices with their start and end apart: 25, of which 13 were waited for; matrix products, arithmetic and copies ran while one was open for 2% of the time, Pallas kernels for 25%

profile of v2, /device:TPU:0, one launch (start us, length us, event | category | flops | bytes accessed | tf_op | source)
XLA Modules:
  0.0 229.6 jit_solution(11515081105341706855)
XLA Ops:
  0.6 1.8 copy.18
  2.5 0.5 call_exported.0.me_ref
  3.0 4.4 %hidden_grad.2.rest_0_ = bf16[8,2,2,16,2048]{4,3,2,1,0:T(8,128)(2,1)} custom-call(s32[2]{0:T(128)} %call_exported.0.me_ref, bf16[512,32]{1,0:T(8,128)(2,1)} %bitcast.15, bf16[1,2048,2048]{2,1,0:T(8,128)(2,1)} %gate_ref.7, bf16[1,2048,2048]{2,1,0:T(8,128)(2,1)} %cot_ref.7), custom_call_target="tpu_custom_call" | custom-call | flops 536870912 | bytes 6291456 | tf_op jit(solution)/shard_map/hidden_grad/pallas_call | solution.py:86
  7.4 5.3 %all-to-all-start = ((bf16[8,2,2,16,2048]{4,3,2,1,0:T(8,128)(2,1)}), bf16[8,2,2,16,2048]{4,3,2,1,0:T(8,128)(2,1)S(1)}, u32[]{:S(2)}, u32[]{:S(2)}) async-start(bf16[8,2,2,16,2048]{4,3,2,1,0:T(8,128)(2,1)} %hidden_grad.2.rest_0_), calls=%async_computation | async-start | bytes 4194304 | tf_op jit(solution)/shard_map/all_to_all | solution.py:356
  12.8 1.5 copy.19
  14.3 0.7 pad_add_fusion.me_ref
  14.9 10.4 %hidden_grad.3 = (bf16[2,6,16,2048]{3,2,1,0:T(8,128)(2,1)}, bf16[2,6,16,2048]{3,2,1,0:T(8,128)(2,1)}, bf16[2,6,16,2048]{3,2,1,0:T(8,128)(2,1)}, bf16[2,6,16,2048...) custom-call(s32[2]{0:T(128)} %pad_add_fusion.me_ref, ...), custom_call_target="tpu_custom_call" | custom-call | flops 1610612736 | bytes 18874368 | tf_op jit(solution)/shard_map/hidden_grad/pallas_call | solution.py:86
  25.3 11.3 %hidden.1 = (bf16[2,6,16,2048]{3,2,1,0:T(8,128)(2,1)}, bf16[2,6,16,2048]{3,2,1,0:T(8,128)(2,1)}, bf16[2,6,16,2048]{3,2,1,0:T(8,128)(2,1)}, bf16[2,6,16,2048]{3,2...) custom-call(s32[2]{0:T(128)} %pad_add_fusion.me_ref, ...), custom_call_target="tpu_custom_call" | custom-call | flops 4294967296 | bytes 16777216 | tf_op jit(solution)/shard_map/hidden/pallas_call | solution.py:134
  36.7 2.7 %all-to-all-done.hg_ref = bf16[8,2,2,16,2048]{4,3,2,1,0:T(8,128)(2,1)S(1)} async-done(((bf16[8,2,2,16,2048]{4,3,2,1,0:T(8,128)(2,1)}), bf16[8,2,2,16,2048]{4,3,2,1,0:T(8,128)(2,1)S(1)}, u32[]{:S(2)}, u32[]{:S(2)}) %all-to-all-start) | async-done | bytes 2097184 | tf_op jit(solution)/shard_map/all_to_all | solution.py:356
  39.4 0.6 collective-permute-start
  40.0 1.4 collective-permute-start.1
  41.4 1.5 collective-permute-start.2
  42.9 1.7 collective-permute-start.4
  44.6 16.4 %collective-permute-done.rest_1_ = bf16[2,6,16,2048]{3,2,1,0:T(8,128)(2,1)S(1)} collective-permute-done((bf16[2,6,16,2048]{3,2,1,0:T(8,128)(2,1)}, bf16[2,6,16,2048]{3,2,1,0:T(8,128)(2,1)S(1)}, u32[]{:S(2)}, u32[]{:S(2)}) %collective-permute-start) | collective-permute-done | bytes 786464 | tf_op jit(solution)/shard_map/ppermute | solution.py:306
  61.0 16.9 %collective-permute-done.1.rest_2_ = bf16[2,6,16,2048]{3,2,1,0:T(8,128)(2,1)S(1)} collective-permute-done((bf16[2,6,16,2048]{3,2,1,0:T(8,128)(2,1)}, bf16[2,6,16,2048]{3,2,1,0:T(8,128)(2,1)S(1)}, u32[]{:S(2)}, u32[]{:S(2)}) %collective-permute-start.1) | collective-permute-done | bytes 786464 | tf_op jit(solution)/shard_map/ppermute | solution.py:306
  77.9 14.1 %collective-permute-done.3.rest_4_ = bf16[2,6,16,2048]{3,2,1,0:T(8,128)(2,1)S(1)} collective-permute-done((bf16[2,6,16,2048]{3,2,1,0:T(8,128)(2,1)}, bf16[2,6,16,2048]{3,2,1,0:T(8,128)(2,1)S(1)}, u32[]{:S(2)}, u32[]{:S(2)}) %collective-permute-start.3) | collective-permute-done | bytes 786464 | tf_op jit(solution)/shard_map/ppermute | solution.py:306
  92.0 16.2 %collective-permute-done.4.rest_5_ = bf16[2,6,16,2048]{3,2,1,0:T(8,128)(2,1)S(1)} collective-permute-done((bf16[2,6,16,2048]{3,2,1,0:T(8,128)(2,1)S(1)}, bf16[2,6,16,2048]{3,2,1,0:T(8,128)(2,1)S(1)}, u32[]{:S(2)}, u32[]{:S(2)}) %collective-permute-start.4) | collective-permute-done | bytes 786464 | tf_op jit(solution)/shard_map/ppermute | solution.py:306
  108.3 1.0 collective-permute-start.7
  109.3 1.5 collective-permute-start.8
  110.8 0.9 collective-permute-start.9
  111.8 0.9 copy-done.12
  112.7 16.8 %block_grads.1 = (bf16[1,2048,2048]{2,1,0:T(8,128)(2,1)}, f32[2,4,128,512]{3,2,1,0:T(8,128)}, bf16[2,4,128,512]{3,2,1,0:T(8,128)(2,1)}) custom-call(s32[2]{0:T(128)} %pad_add_fusion.me_ref, bf16[4,512,512]{2,1,0:T(8,128)(2,1)} %f_ref.3, bf16[1,2048,2048]{2,1,0:T(8,128)(2,1)} %x_ref.3, bf16[8,2,2,16,2048]{4,3,2,1,0:T(8,128)(2,1)} %copy-done, ...), custom_call_target="tpu_custom_call" | custom-call | flops 8589934592 | bytes 25165824 | tf_op jit(solution)/shard_map/block_grads/pallas_call | solution.py:198
  129.5 0.3 collective-permute-done.7.rest_1_
  129.8 16.1 %collective-permute-done.8.rest_2_ = bf16[2,6,16,2048]{3,2,1,0:T(8,128)(2,1)} collective-permute-done((bf16[2,6,16,2048]{3,2,1,0:T(8,128)(2,1)}, bf16[2,6,16,2048]{3,2,1,0:T(8,128)(2,1)}, u32[]{:S(2)}, u32[]{:S(2)}) %collective-permute-start.8) | collective-permute-done | bytes 786464 | tf_op jit(solution)/shard_map/ppermute | solution.py:306
  146.1 1.6 collective-permute-start.21
  147.7 0.8 collective-permute-start.16
  148.5 1.9 collective-permute-start.17
  150.4 0.6 collective-permute-start.19
  151.0 20.3 %collective-permute-done.21 = bf16[2,4,128,512]{3,2,1,0:T(8,128)(2,1)S(1)} collective-permute-done((bf16[2,4,128,512]{3,2,1,0:T(8,128)(2,1)}, bf16[2,4,128,512]{3,2,1,0:T(8,128)(2,1)S(1)}, u32[]{:S(2)}, u32[]{:S(2)}) %collective-permute-start.21) | collective-permute-done | bytes 1048608 | tf_op jit(solution)/shard_map/ppermute | solution.py:311
  171.3 1.6 collective-permute-start.10
  172.9 2.0 convert_add_fusion
  175.0 1.6 collective-permute-start.11
  176.6 8.8 %collective-permute-done.17.rest_5_ = bf16[2,6,16,2048]{3,2,1,0:T(8,128)(2,1)} collective-permute-done((bf16[2,6,16,2048]{3,2,1,0:T(8,128)(2,1)}, bf16[2,6,16,2048]{3,2,1,0:T(8,128)(2,1)}, u32[]{:S(2)}, u32[]{:S(2)}) %collective-permute-start.17) | collective-permute-done | bytes 786464 | tf_op jit(solution)/shard_map/ppermute | solution.py:306
  185.4 1.5 collective-permute-start.12
  186.9 1.1 collective-permute-start.13
  187.9 2.6 %collective-permute-start.22 = (bf16[1,4,128,512]{3,2,1,0:T(8,128)(2,1)S(1)}, bf16[1,4,128,512]{3,2,1,0:T(8,128)(2,1)S(1)}, u32[]{:S(2)}, u32[]{:S(2)}) collective-permute-start(bf16[1,4,128,512]{3,2,1,0:T(8,128)(2,1)S(1)} %slice.21), channel_id=1, source_target_pairs={{0,16},{8,24},{16,0},{24,8},{1,17},{9,25},{17,1},{25,9},{2,18},{10... | collective-permute-start | bytes 1572872 | tf_op jit(solution)/shard_map/ppermute | solution.py:311
  190.5 12.7 %mixed.2 = (bf16[1,2048,2048]{2,1,0:T(8,128)(2,1)}, bf16[4,8,16,128]{3,2,1,0:T(8,128)(2,1)}) custom-call(s32[2]{0:T(128)} %pad_add_fusion.me_ref, bf16[2048,32]{1,0:T(8,128)(2,1)} %bitcast.11, bf16[1,2048,2048]{2,1,0:T(8,128)(2,1)} %gate_ref.7, bf16[1,2048,2048]{2,1,0:T(8,128)(2,1)} %cot_ref.7, bf16[2,6,16,2048]{3,2,1,0:T(8,128)(2,1)} %get-tuple-element.145.rest_0_, ...), custom_call_target="tpu_custom_call" | custom-call | flops 3221225472 | bytes 25165824 | tf_op jit(solution)/shard_map/mixed/pallas_call | solution.py:270
  203.2 0.4 collective-permute-start.14
  203.7 1.5 collective-permute-start.15
  205.3 6.5 %collective-permute-done.14.rest_5_ = bf16[2,2,16,2048]{3,2,1,0:T(8,128)(2,1)} collective-permute-done((bf16[2,2,16,2048]{3,2,1,0:T(8,128)(2,1)}, bf16[2,2,16,2048]{3,2,1,0:T(8,128)(2,1)}, u32[]{:S(2)}, u32[]{:S(2)}) %collective-permute-start.14) | collective-permute-done | bytes 262176 | tf_op jit(solution)/shard_map/ppermute | solution.py:306
  211.8 0.3 collective-permute-done.15.rest_6_
  212.2 5.9 %mixed.3 = (bf16[1,2048,2048]{2,1,0:T(8,128)(2,1)}, bf16[4,8,16,128]{3,2,1,0:T(8,128)(2,1)}) custom-call(s32[2]{0:T(128)} %pad_add_fusion.me_ref, bf16[2048,32]{1,0:T(8,128)(2,1)} %bitcast.12, bf16[1,2048,2048]{2,1,0:T(8,128)(2,1)} %gate_ref.7, bf16[1,2048,2048]{2,1,0:T(8,128)(2,1)} %cot_ref.7, ...), custom_call_target="tpu_custom_call", output_to_operand_aliasing={{0}: (12, {}), {1}: (13, {})} | custom-call | flops 1073741824 | bytes 8388608 | tf_op jit(solution)/shard_map/mixed/pallas_call | solution.py:270
  218.1 3.3 %all-to-all-start.1 = ((bf16[4,8,16,128]{3,2,1,0:T(8,128)(2,1)}), bf16[4,8,16,128]{3,2,1,0:T(8,128)(2,1)S(1)}, u32[]{:S(2)}, u32[]{:S(2)}) async-start(bf16[4,8,16,128]{3,2,1,0:T(8,128)(2,1)} %get-tuple-element.165), calls=%async_computation.1 | async-start | bytes 262144 | tf_op jit(solution)/shard_map/all_to_all | solution.py:333
  221.4 1.2 fusion
  222.6 5.3 %all-to-all-done.1 = bf16[4,8,16,128]{3,2,1,0:T(8,128)(2,1)S(1)} async-done(((bf16[4,8,16,128]{3,2,1,0:T(8,128)(2,1)}), bf16[4,8,16,128]{3,2,1,0:T(8,128)(2,1)S(1)}, u32[]{:S(2)}, u32[]{:S(2)}) %all-to-all-start.1) | async-done | bytes 131104 | tf_op jit(solution)/shard_map/all_to_all | solution.py:333
  228.1 0.4 copy.21
  228.5 0.3 reshape.23
  228.8 0.8 copy.22
  (46 shorter events, 0.8 us)
Async XLA Ops:
  7.4 5.3 %copy-start.1 = (bf16[64,32,32]{0,2,1:T(8,128)(2,1)S(1)}, bf16[64,32,32]{0,2,1:T(8,128)(2,1)}, u32[]{:S(2)}) copy-start(bf16[64,32,32]{0,2,1:T(8,128)(2,1)} %param.10) | copy-start | bytes 393220
  7.4 32.0 %all-to-all-start = ((bf16[8,2,2,16,2048]{4,3,2,1,0:T(8,128)(2,1)}), bf16[8,2,2,16,2048]{4,3,2,1,0:T(8,128)(2,1)S(1)}, u32[]{:S(2)}, u32[]{:S(2)}) async-start(bf16[8,2,2,16,2048]{4,3,2,1,0:T(8,128)(2,1)} %hidden_grad.2.rest_0_), calls=%async_computation | async-start | bytes 4194304 | tf_op jit(solution)/shard_map/all_to_all | solution.py:356
  25.3 17.5 %copy-start.6 = (bf16[2,6,16,2048]{3,2,1,0:T(8,128)(2,1)S(1)}, bf16[2,6,16,2048]{3,2,1,0:T(8,128)(2,1)}, u32[]{:S(2)}) copy-start(bf16[2,6,16,2048]{3,2,1,0:T(8,128)(2,1)} %get-tuple-element.117) | copy-start | bytes 2359300
  39.4 73.3 %copy-start = (bf16[8,2,2,16,2048]{4,3,2,1,0:T(8,128)(2,1)}, bf16[8,2,2,16,2048]{4,3,2,1,0:T(8,128)(2,1)S(1)}, u32[]{:S(2)}) copy-start(bf16[8,2,2,16,2048]{4,3,2,1,0:T(8,128)(2,1)S(1)} %all-to-all-done.hg_ref) | copy-start | bytes 6291460
  39.4 21.6 %collective-permute-start = (bf16[2,6,16,2048]{3,2,1,0:T(8,128)(2,1)}, bf16[2,6,16,2048]{3,2,1,0:T(8,128)(2,1)S(1)}, u32[]{:S(2)}, u32[]{:S(2)}) collective-permute-start(bf16[2,6,16,2048]{3,2,1,0:T(8,128)(2,1)} %get-tuple-element.113), channel_id=1, source_target_pairs={{0,6},{1,7},{2,4},{3,5},{4,2},{5,3},{6,0},{7,1},{8,14},{9,15},{10,... | collective-permute-start | bytes 2359304 | tf_op jit(solution)/shard_map/ppermute | solution.py:306
  40.0 37.9 %collective-permute-start.1 = (bf16[2,6,16,2048]{3,2,1,0:T(8,128)(2,1)}, bf16[2,6,16,2048]{3,2,1,0:T(8,128)(2,1)S(1)}, u32[]{:S(2)}, u32[]{:S(2)}) collective-permute-start(bf16[2,6,16,2048]{3,2,1,0:T(8,128)(2,1)} %get-tuple-element.114), channel_id=1, source_target_pairs={{0,4},{1,5},{2,6},{3,7},{4,0},{5,1},{6,2},{7,3},{8,12},{9,13},{10,... | collective-permute-start | bytes 2359304 | tf_op jit(solution)/shard_map/ppermute | solution.py:306
  41.4 36.6 %collective-permute-start.2 = (bf16[2,6,16,2048]{3,2,1,0:T(8,128)(2,1)}, bf16[2,6,16,2048]{3,2,1,0:T(8,128)(2,1)S(1)}, u32[]{:S(2)}, u32[]{:S(2)}) collective-permute-start(bf16[2,6,16,2048]{3,2,1,0:T(8,128)(2,1)} %get-tuple-element.115), channel_id=1, source_target_pairs={{0,2},{1,3},{2,0},{3,1},{4,6},{5,7},{6,4},{7,5},{8,10},{9,11},{10,... | collective-permute-start | bytes 2359304 | tf_op jit(solution)/shard_map/ppermute | solution.py:306
  42.9 49.1 %collective-permute-start.3 = (bf16[2,6,16,2048]{3,2,1,0:T(8,128)(2,1)}, bf16[2,6,16,2048]{3,2,1,0:T(8,128)(2,1)S(1)}, u32[]{:S(2)}, u32[]{:S(2)}) collective-permute-start(bf16[2,6,16,2048]{3,2,1,0:T(8,128)(2,1)} %get-tuple-element.116), channel_id=1, source_target_pairs={{0,7},{1,6},{2,5},{3,4},{4,3},{5,2},{6,1},{7,0},{8,15},{9,14},{10,... | collective-permute-start | bytes 2359304 | tf_op jit(solution)/shard_map/ppermute | solution.py:306
  42.9 65.4 %collective-permute-start.4 = (bf16[2,6,16,2048]{3,2,1,0:T(8,128)(2,1)S(1)}, bf16[2,6,16,2048]{3,2,1,0:T(8,128)(2,1)S(1)}, u32[]{:S(2)}, u32[]{:S(2)}) collective-permute-start(bf16[2,6,16,2048]{3,2,1,0:T(8,128)(2,1)S(1)} %copy-done.6), channel_id=1, source_target_pairs={{0,5},{1,4},{2,7},{3,6},{4,1},{5,0},{6,3},{7,2},{8,13},{9,12},{10,... | collective-permute-start | bytes 2359304 | tf_op jit(solution)/shard_map/ppermute | solution.py:306
  61.0 47.3 %copy-start.7 = (bf16[2,6,16,2048]{3,2,1,0:T(8,128)(2,1)}, bf16[2,6,16,2048]{3,2,1,0:T(8,128)(2,1)S(1)}, u32[]{:S(2)}) copy-start(bf16[2,6,16,2048]{3,2,1,0:T(8,128)(2,1)S(1)} %collective-permute-done.rest_1_) | copy-start | bytes 2359300
  61.0 50.8 %collective-permute-start.5 = (bf16[2,6,16,2048]{3,2,1,0:T(8,128)(2,1)}, bf16[2,6,16,2048]{3,2,1,0:T(8,128)(2,1)S(1)}, u32[]{:S(2)}, u32[]{:S(2)}) collective-permute-start(bf16[2,6,16,2048]{3,2,1,0:T(8,128)(2,1)} %get-tuple-element.123), channel_id=1, source_target_pairs={{0,3},{1,2},{2,1},{3,0},{4,7},{5,6},{6,5},{7,4},{8,11},{9,10},{10,... | collective-permute-start | bytes 2359304 | tf_op jit(solution)/shard_map/ppermute | solution.py:306
  77.9 31.4 %copy-start.8 = (bf16[2,6,16,2048]{3,2,1,0:T(8,128)(2,1)}, bf16[2,6,16,2048]{3,2,1,0:T(8,128)(2,1)S(1)}, u32[]{:S(2)}) copy-start(bf16[2,6,16,2048]{3,2,1,0:T(8,128)(2,1)S(1)} %collective-permute-done.1.rest_2_) | copy-start | bytes 2359300
  77.9 34.8 %collective-permute-start.6 = (bf16[2,6,16,2048]{3,2,1,0:T(8,128)(2,1)}, bf16[2,6,16,2048]{3,2,1,0:T(8,128)(2,1)}, u32[]{:S(2)}, u32[]{:S(2)}) collective-permute-start(bf16[2,6,16,2048]{3,2,1,0:T(8,128)(2,1)} %get-tuple-element.124), channel_id=1, source_target_pairs={{0,1},{1,0},{2,3},{3,2},{4,5},{5,4},{6,7},{7,6},{8,9},{9,8},{10,11... | collective-permute-start | bytes 2359304 | tf_op jit(solution)/shard_map/ppermute | solution.py:306
  77.9 32.9 %copy-start.9 = (bf16[2,6,16,2048]{3,2,1,0:T(8,128)(2,1)}, bf16[2,6,16,2048]{3,2,1,0:T(8,128)(2,1)S(1)}, u32[]{:S(2)}) copy-start(bf16[2,6,16,2048]{3,2,1,0:T(8,128)(2,1)S(1)} %collective-permute-done.2.rest_3_) | copy-start | bytes 2359300
  92.0 19.8 %copy-start.10 = (bf16[2,6,16,2048]{3,2,1,0:T(8,128)(2,1)}, bf16[2,6,16,2048]{3,2,1,0:T(8,128)(2,1)S(1)}, u32[]{:S(2)}) copy-start(bf16[2,6,16,2048]{3,2,1,0:T(8,128)(2,1)S(1)} %collective-permute-done.3.rest_4_) | copy-start | bytes 2359300
  108.3 3.5 %copy-start.11 = (bf16[2,6,16,2048]{3,2,1,0:T(8,128)(2,1)}, bf16[2,6,16,2048]{3,2,1,0:T(8,128)(2,1)S(1)}, u32[]{:S(2)}) copy-start(bf16[2,6,16,2048]{3,2,1,0:T(8,128)(2,1)S(1)} %collective-permute-done.4.rest_5_) | copy-start | bytes 2359300
  108.3 21.5 %collective-permute-start.7 = (bf16[2,6,16,2048]{3,2,1,0:T(8,128)(2,1)}, bf16[2,6,16,2048]{3,2,1,0:T(8,128)(2,1)S(1)}, u32[]{:S(2)}, u32[]{:S(2)}) collective-permute-start(bf16[2,6,16,2048]{3,2,1,0:T(8,128)(2,1)} %get-tuple-element.134), channel_id=1, source_target_pairs={{0,6},{1,7},{2,4},{3,5},{4,2},{5,3},{6,0},{7,1},{8,14},{9,15},{10,... | collective-permute-start | bytes 2359304 | tf_op jit(solution)/shard_map/ppermute | solution.py:306
  109.3 36.6 %collective-permute-start.8 = (bf16[2,6,16,2048]{3,2,1,0:T(8,128)(2,1)}, bf16[2,6,16,2048]{3,2,1,0:T(8,128)(2,1)}, u32[]{:S(2)}, u32[]{:S(2)}) collective-permute-start(bf16[2,6,16,2048]{3,2,1,0:T(8,128)(2,1)} %get-tuple-element.135), channel_id=1, source_target_pairs={{0,4},{1,5},{2,6},{3,7},{4,0},{5,1},{6,2},{7,3},{8,12},{9,13},{10,... | collective-permute-start | bytes 2359304 | tf_op jit(solution)/shard_map/ppermute | solution.py:306
  110.8 35.3 %collective-permute-start.9 = (bf16[2,6,16,2048]{3,2,1,0:T(8,128)(2,1)}, bf16[2,6,16,2048]{3,2,1,0:T(8,128)(2,1)}, u32[]{:S(2)}, u32[]{:S(2)}) collective-permute-start(bf16[2,6,16,2048]{3,2,1,0:T(8,128)(2,1)} %get-tuple-element.136), channel_id=1, source_target_pairs={{0,2},{1,3},{2,0},{3,1},{4,6},{5,7},{6,4},{7,5},{8,10},{9,11},{10,... | collective-permute-start | bytes 2359304 | tf_op jit(solution)/shard_map/ppermute | solution.py:306
  111.8 0.9 copy-start.12
  129.8 45.1 %copy-start.2 = (bf16[2,6,16,2048]{3,2,1,0:T(8,128)(2,1)}, bf16[2,6,16,2048]{3,2,1,0:T(8,128)(2,1)S(1)}, u32[]{:S(2)}) copy-start(bf16[2,6,16,2048]{3,2,1,0:T(8,128)(2,1)S(1)} %collective-permute-done.7.rest_1_) | copy-start | bytes 2359300
  146.1 25.1 %collective-permute-start.21 = (bf16[2,4,128,512]{3,2,1,0:T(8,128)(2,1)}, bf16[2,4,128,512]{3,2,1,0:T(8,128)(2,1)S(1)}, u32[]{:S(2)}, u32[]{:S(2)}) collective-permute-start(bf16[2,4,128,512]{3,2,1,0:T(8,128)(2,1)} %get-tuple-element.156.rest_8_), channel_id=1, source_target_pairs={{0,8},{8,0},{16,24},{24,16},{1,9},{9,1},{17,25},{25,17},{2,10},{10... | collective-permute-start | bytes 3145736 | tf_op jit(solution)/shard_map/ppermute | solution.py:311
  147.7 27.3 %collective-permute-start.16 = (bf16[2,6,16,2048]{3,2,1,0:T(8,128)(2,1)}, bf16[2,6,16,2048]{3,2,1,0:T(8,128)(2,1)}, u32[]{:S(2)}, u32[]{:S(2)}) collective-permute-start(bf16[2,6,16,2048]{3,2,1,0:T(8,128)(2,1)} %get-tuple-element.152), channel_id=1, source_target_pairs={{0,7},{1,6},{2,5},{3,4},{4,3},{5,2},{6,1},{7,0},{8,15},{9,14},{10,... | collective-permute-start | bytes 2359304 | tf_op jit(solution)/shard_map/ppermute | solution.py:306
  148.5 36.9 %collective-permute-start.17 = (bf16[2,6,16,2048]{3,2,1,0:T(8,128)(2,1)}, bf16[2,6,16,2048]{3,2,1,0:T(8,128)(2,1)}, u32[]{:S(2)}, u32[]{:S(2)}) collective-permute-start(bf16[2,6,16,2048]{3,2,1,0:T(8,128)(2,1)} %get-tuple-element.153), channel_id=1, source_target_pairs={{0,5},{1,4},{2,7},{3,6},{4,1},{5,0},{6,3},{7,2},{8,13},{9,12},{10,... | collective-permute-start | bytes 2359304 | tf_op jit(solution)/shard_map/ppermute | solution.py:306
  150.4 36.5 %collective-permute-start.18 = (bf16[2,6,16,2048]{3,2,1,0:T(8,128)(2,1)}, bf16[2,6,16,2048]{3,2,1,0:T(8,128)(2,1)}, u32[]{:S(2)}, u32[]{:S(2)}) collective-permute-start(bf16[2,6,16,2048]{3,2,1,0:T(8,128)(2,1)} %get-tuple-element.154), channel_id=1, source_target_pairs={{0,3},{1,2},{2,1},{3,0},{4,7},{5,6},{6,5},{7,4},{8,11},{9,10},{10,... | collective-permute-start | bytes 2359304 | tf_op jit(solution)/shard_map/ppermute | solution.py:306
  150.4 37.5 %collective-permute-start.19 = (bf16[2,6,16,2048]{3,2,1,0:T(8,128)(2,1)}, bf16[2,6,16,2048]{3,2,1,0:T(8,128)(2,1)}, u32[]{:S(2)}, u32[]{:S(2)}) collective-permute-start(bf16[2,6,16,2048]{3,2,1,0:T(8,128)(2,1)} %get-tuple-element.155), channel_id=1, source_target_pairs={{0,1},{1,0},{2,3},{3,2},{4,5},{5,4},{6,7},{7,6},{8,9},{9,8},{10,11... | collective-permute-start | bytes 2359304 | tf_op jit(solution)/shard_map/ppermute | solution.py:306
  171.3 32.0 %collective-permute-start.10 = (bf16[2,2,16,2048]{3,2,1,0:T(8,128)(2,1)}, bf16[2,2,16,2048]{3,2,1,0:T(8,128)(2,1)S(1)}, u32[]{:S(2)}, u32[]{:S(2)}) collective-permute-start(bf16[2,2,16,2048]{3,2,1,0:T(8,128)(2,1)} %get-tuple-element.138), channel_id=1, source_target_pairs={{0,6},{1,7},{2,4},{3,5},{4,2},{5,3},{6,0},{7,1},{8,14},{9,15},{10,... | collective-permute-start | bytes 786440 | tf_op jit(solution)/shard_map/ppermute | solution.py:306
  175.0 28.7 %collective-permute-start.11 = (bf16[2,2,16,2048]{3,2,1,0:T(8,128)(2,1)}, bf16[2,2,16,2048]{3,2,1,0:T(8,128)(2,1)S(1)}, u32[]{:S(2)}, u32[]{:S(2)}) collective-permute-start(bf16[2,2,16,2048]{3,2,1,0:T(8,128)(2,1)} %get-tuple-element.139), channel_id=1, source_target_pairs={{0,4},{1,5},{2,6},{3,7},{4,0},{5,1},{6,2},{7,3},{8,12},{9,13},{10,... | collective-permute-start | bytes 786440 | tf_op jit(solution)/shard_map/ppermute | solution.py:306
  185.4 19.8 %collective-permute-start.12 = (bf16[2,2,16,2048]{3,2,1,0:T(8,128)(2,1)}, bf16[2,2,16,2048]{3,2,1,0:T(8,128)(2,1)S(1)}, u32[]{:S(2)}, u32[]{:S(2)}) collective-permute-start(bf16[2,2,16,2048]{3,2,1,0:T(8,128)(2,1)} %get-tuple-element.140), channel_id=1, source_target_pairs={{0,2},{1,3},{2,0},{3,1},{4,6},{5,7},{6,4},{7,5},{8,10},{9,11},{10,... | collective-permute-start | bytes 786440 | tf_op jit(solution)/shard_map/ppermute | solution.py:306
  186.9 18.5 %collective-permute-start.13 = (bf16[2,2,16,2048]{3,2,1,0:T(8,128)(2,1)}, bf16[2,2,16,2048]{3,2,1,0:T(8,128)(2,1)}, u32[]{:S(2)}, u32[]{:S(2)}) collective-permute-start(bf16[2,2,16,2048]{3,2,1,0:T(8,128)(2,1)} %get-tuple-element.141), channel_id=1, source_target_pairs={{0,7},{1,6},{2,5},{3,4},{4,3},{5,2},{6,1},{7,0},{8,15},{9,14},{10,... | collective-permute-start | bytes 786440 | tf_op jit(solution)/shard_map/ppermute | solution.py:306
  187.9 30.2 %collective-permute-start.22 = (bf16[1,4,128,512]{3,2,1,0:T(8,128)(2,1)S(1)}, bf16[1,4,128,512]{3,2,1,0:T(8,128)(2,1)S(1)}, u32[]{:S(2)}, u32[]{:S(2)}) collective-permute-start(bf16[1,4,128,512]{3,2,1,0:T(8,128)(2,1)S(1)} %slice.21), channel_id=1, source_target_pairs={{0,16},{8,24},{16,0},{24,8},{1,17},{9,25},{17,1},{25,9},{2,18},{10... | collective-permute-start | bytes 1572872 | tf_op jit(solution)/shard_map/ppermute | solution.py:311
  203.2 8.9 %copy-start.3 = (bf16[2,2,16,2048]{3,2,1,0:T(8,128)(2,1)}, bf16[2,2,16,2048]{3,2,1,0:T(8,128)(2,1)S(1)}, u32[]{:S(2)}) copy-start(bf16[2,2,16,2048]{3,2,1,0:T(8,128)(2,1)S(1)} %collective-permute-done.10.rest_1_) | copy-start | bytes 786436
  203.2 8.6 %collective-permute-start.14 = (bf16[2,2,16,2048]{3,2,1,0:T(8,128)(2,1)}, bf16[2,2,16,2048]{3,2,1,0:T(8,128)(2,1)}, u32[]{:S(2)}, u32[]{:S(2)}) collective-permute-start(bf16[2,2,16,2048]{3,2,1,0:T(8,128)(2,1)} %get-tuple-element.142), channel_id=1, source_target_pairs={{0,5},{1,4},{2,7},{3,6},{4,1},{5,0},{6,3},{7,2},{8,13},{9,12},{10,... | collective-permute-start | bytes 786440 | tf_op jit(solution)/shard_map/ppermute | solution.py:306
  203.7 8.5 %copy-start.4 = (bf16[2,2,16,2048]{3,2,1,0:T(8,128)(2,1)}, bf16[2,2,16,2048]{3,2,1,0:T(8,128)(2,1)S(1)}, u32[]{:S(2)}) copy-start(bf16[2,2,16,2048]{3,2,1,0:T(8,128)(2,1)S(1)} %collective-permute-done.11.rest_2_) | copy-start | bytes 786436
  203.7 8.5 %collective-permute-start.15 = (bf16[2,2,16,2048]{3,2,1,0:T(8,128)(2,1)}, bf16[2,2,16,2048]{3,2,1,0:T(8,128)(2,1)}, u32[]{:S(2)}, u32[]{:S(2)}) collective-permute-start(bf16[2,2,16,2048]{3,2,1,0:T(8,128)(2,1)} %get-tuple-element.143), channel_id=1, source_target_pairs={{0,3},{1,2},{2,1},{3,0},{4,7},{5,6},{6,5},{7,4},{8,11},{9,10},{10,... | collective-permute-start | bytes 786440 | tf_op jit(solution)/shard_map/ppermute | solution.py:306
  205.2 7.0 %copy-start.5 = (bf16[2,2,16,2048]{3,2,1,0:T(8,128)(2,1)}, bf16[2,2,16,2048]{3,2,1,0:T(8,128)(2,1)S(1)}, u32[]{:S(2)}) copy-start(bf16[2,2,16,2048]{3,2,1,0:T(8,128)(2,1)S(1)} %collective-permute-done.12.rest_3_) | copy-start | bytes 786436
  205.2 7.0 %collective-permute-start.20 = (bf16[2,2,16,2048]{3,2,1,0:T(8,128)(2,1)}, bf16[2,2,16,2048]{3,2,1,0:T(8,128)(2,1)}, u32[]{:S(2)}, u32[]{:S(2)}) collective-permute-start(bf16[2,2,16,2048]{3,2,1,0:T(8,128)(2,1)} %get-tuple-element.158), channel_id=1, source_target_pairs={{0,1},{1,0},{2,3},{3,2},{4,5},{5,4},{6,7},{7,6},{8,9},{9,8},{10,11... | collective-permute-start | bytes 786440 | tf_op jit(solution)/shard_map/ppermute | solution.py:306
  218.1 9.8 %all-to-all-start.1 = ((bf16[4,8,16,128]{3,2,1,0:T(8,128)(2,1)}), bf16[4,8,16,128]{3,2,1,0:T(8,128)(2,1)S(1)}, u32[]{:S(2)}, u32[]{:S(2)}) async-start(bf16[4,8,16,128]{3,2,1,0:T(8,128)(2,1)} %get-tuple-element.165), calls=%async_computation.1 | async-start | bytes 262144 | tf_op jit(solution)/shard_map/all_to_all | solution.py:333

commit v3 on v2

--- a/solution.py
+++ b/solution.py
@@ -224,7 +224,7 @@
 
 def mixed_kernel(nseq, ndp, lb, nb, factor, me_ref, s_ref, gate_ref, cot_ref, *rest):
     hs = dict(zip([0] + _wire_order(nseq), rest[:nseq]))
-    gg_ref, out, pick, mask, order, choose, m, hid, mg = rest[-9:]
+    gg_ref, out, pick, mask, flat, order, choose, m, hid, mg = rest[-10:]
     rows, cols = nb * G, G * nb
     share = nb // ndp
     width = gg_ref.shape[2]
@@ -234,6 +234,8 @@
         pick[...] = _pick(nb, lb, me_ref[0])
         same = _iota((cols, rows), 1) % G == _iota((cols, rows), 0) // nb
         mask[...] = same.astype(F32)
+        same = _iota((rows, cols), 0) % G == _iota((rows, cols), 1) // nb
+        flat[...] = same.astype(F32) * factor
         r = _iota((nb, nb), 1)
         block = jnp.bitwise_xor(r // lb, me_ref[0]) * lb + r % lb
         order[...] = (block == _iota((nb, nb), 0)).astype(BF16)
@@ -248,8 +250,8 @@
         mixed = _dot(m[...], hid[:, c:c + 256])
         gg_ref[0, :, c:c + 256] = (cot.astype(F32) * mixed).astype(BF16)
         mg[:, c:c + 256] = cot * gate_ref[0, :, c:c + 256]
-    kept = _dot_nt(mg[...], hid[...]) * mask[...]
-    terms = jnp.sum(kept.T.reshape(nb, G, cols), axis=1) * factor
+    kept = _dot_nt(hid[...], mg[...]) * flat[...]
+    terms = jnp.sum(kept.reshape(nb, G, cols), axis=1)
     terms = _dot(order[...], terms.astype(BF16)).astype(BF16)
     terms = _dot(terms, choose[...])
     tall = out.shape[2]
@@ -280,6 +282,7 @@
         [
             pltpu.VMEM((nb * G, nb), BF16),
             pltpu.VMEM(square, F32),
+            pltpu.VMEM(square, F32),
             pltpu.VMEM((nb, nb), BF16),
             pltpu.VMEM((G * nb, G * nb), BF16),
             pltpu.VMEM(square, BF16),

time: 230 us -> 230 us (level)
  no operation moved by 1% of the time
where the time goes in v3:
time: 230 us; the launch traced here: 229 us
  waiting for transfers between devices  124 us (54%)
  Pallas kernels  61.2 us (27%)
  starting transfers between devices  32.6 us (14%)
  local copies, waits for them, and re-layouts  6.57 us (3%)
  other arithmetic  3.83 us (2%)
    ppermute x21, waiting for transfers between devices, _swap(): got[k] = lax.ppermute(parts[k], axis, [(s, s ^ k) for s in range(size)])  96 us
    ppermute x2, waiting for transfers between devices, _pass(): return lax.ppermute(part, axis, [(z, z ^ step) for z in range(size)])  20.3 us
    ppermute x21, starting transfers between devices, _swap(): got[k] = lax.ppermute(parts[k], axis, [(s, s ^ k) for s in range(size)])  19.8 us
    pallas_call x2, Pallas kernels, mixed_stage(): _call(functools.partial(mixed_kernel, nseq, ndp, lb, nb, factor), (ng,),...  18.2 us
    pallas_call x1, Pallas kernels, block_grads(): _call(functools.partial(block_grads_kernel, nseq, ndp, lo, factor), (lb /...  16.8 us
    pallas_call x2, Pallas kernels, hidden_grad(): _call(functools.partial(hidden_grad_kernel, nseq, lb, nb, split), (ng,),...  14.8 us
    pallas_call x1, Pallas kernels, hidden_forward(): _call(functools.partial(hidden_kernel, nseq, lo, spans), (lb // 2, width...  11.3 us
    all_to_all x1, starting transfers between devices, local(): lax.all_to_all(back_a, 'seq', split_axis=0, concat_axis=0, tiled=True)  5.32 us
  transfers between devices with their start and end apart: 25, of which 13 were waited for; matrix products, arithmetic and copies ran while one was open for 2% of the time, Pallas kernels for 25%

profile of v3, /device:TPU:0, one launch (start us, length us, event | category | flops | bytes accessed | tf_op | source)
XLA Modules:
  0.0 229.2 jit_solution(18304651072166712581)
XLA Ops:
  0.6 1.8 copy.18
  2.5 0.5 call_exported.0.me_ref
  3.0 4.4 %hidden_grad.2.rest_0_ = bf16[8,2,2,16,2048]{4,3,2,1,0:T(8,128)(2,1)} custom-call(s32[2]{0:T(128)} %call_exported.0.me_ref, bf16[512,32]{1,0:T(8,128)(2,1)} %bitcast.15, bf16[1,2048,2048]{2,1,0:T(8,128)(2,1)} %gate_ref.7, bf16[1,2048,2048]{2,1,0:T(8,128)(2,1)} %cot_ref.7), custom_call_target="tpu_custom_call" | custom-call | flops 536870912 | bytes 6291456 | tf_op jit(solution)/shard_map/hidden_grad/pallas_call | solution.py:86
  7.4 5.3 %all-to-all-start = ((bf16[8,2,2,16,2048]{4,3,2,1,0:T(8,128)(2,1)}), bf16[8,2,2,16,2048]{4,3,2,1,0:T(8,128)(2,1)S(1)}, u32[]{:S(2)}, u32[]{:S(2)}) async-start(bf16[8,2,2,16,2048]{4,3,2,1,0:T(8,128)(2,1)} %hidden_grad.2.rest_0_), calls=%async_computation | async-start | bytes 4194304 | tf_op jit(solution)/shard_map/all_to_all | solution.py:359
  12.8 1.5 copy.19
  14.3 0.7 pad_add_fusion.me_ref
  14.9 10.4 %hidden_grad.3 = (bf16[2,6,16,2048]{3,2,1,0:T(8,128)(2,1)}, bf16[2,6,16,2048]{3,2,1,0:T(8,128)(2,1)}, bf16[2,6,16,2048]{3,2,1,0:T(8,128)(2,1)}, bf16[2,6,16,2048...) custom-call(s32[2]{0:T(128)} %pad_add_fusion.me_ref, ...), custom_call_target="tpu_custom_call" | custom-call | flops 1610612736 | bytes 18874368 | tf_op jit(solution)/shard_map/hidden_grad/pallas_call | solution.py:86
  25.3 11.3 %hidden.1 = (bf16[2,6,16,2048]{3,2,1,0:T(8,128)(2,1)}, bf16[2,6,16,2048]{3,2,1,0:T(8,128)(2,1)}, bf16[2,6,16,2048]{3,2,1,0:T(8,128)(2,1)}, bf16[2,6,16,2048]{3,2...) custom-call(s32[2]{0:T(128)} %pad_add_fusion.me_ref, ...), custom_call_target="tpu_custom_call" | custom-call | flops 4294967296 | bytes 16777216 | tf_op jit(solution)/shard_map/hidden/pallas_call | solution.py:134
  36.7 2.7 %all-to-all-done.hg_ref = bf16[8,2,2,16,2048]{4,3,2,1,0:T(8,128)(2,1)S(1)} async-done(((bf16[8,2,2,16,2048]{4,3,2,1,0:T(8,128)(2,1)}), bf16[8,2,2,16,2048]{4,3,2,1,0:T(8,128)(2,1)S(1)}, u32[]{:S(2)}, u32[]{:S(2)}) %all-to-all-start) | async-done | bytes 2097184 | tf_op jit(solution)/shard_map/all_to_all | solution.py:359
  39.4 0.6 collective-permute-start
  40.0 1.4 collective-permute-start.1
  41.4 1.5 collective-permute-start.2
  42.9 1.7 collective-permute-start.4
  44.6 16.4 %collective-permute-done.rest_1_ = bf16[2,6,16,2048]{3,2,1,0:T(8,128)(2,1)S(1)} collective-permute-done((bf16[2,6,16,2048]{3,2,1,0:T(8,128)(2,1)}, bf16[2,6,16,2048]{3,2,1,0:T(8,128)(2,1)S(1)}, u32[]{:S(2)}, u32[]{:S(2)}) %collective-permute-start) | collective-permute-done | bytes 786464 | tf_op jit(solution)/shard_map/ppermute | solution.py:309
  61.0 16.9 %collective-permute-done.1.rest_2_ = bf16[2,6,16,2048]{3,2,1,0:T(8,128)(2,1)S(1)} collective-permute-done((bf16[2,6,16,2048]{3,2,1,0:T(8,128)(2,1)}, bf16[2,6,16,2048]{3,2,1,0:T(8,128)(2,1)S(1)}, u32[]{:S(2)}, u32[]{:S(2)}) %collective-permute-start.1) | collective-permute-done | bytes 786464 | tf_op jit(solution)/shard_map/ppermute | solution.py:309
  77.9 14.1 %collective-permute-done.3.rest_4_ = bf16[2,6,16,2048]{3,2,1,0:T(8,128)(2,1)S(1)} collective-permute-done((bf16[2,6,16,2048]{3,2,1,0:T(8,128)(2,1)}, bf16[2,6,16,2048]{3,2,1,0:T(8,128)(2,1)S(1)}, u32[]{:S(2)}, u32[]{:S(2)}) %collective-permute-start.3) | collective-permute-done | bytes 786464 | tf_op jit(solution)/shard_map/ppermute | solution.py:309
  92.0 16.2 %collective-permute-done.4.rest_5_ = bf16[2,6,16,2048]{3,2,1,0:T(8,128)(2,1)S(1)} collective-permute-done((bf16[2,6,16,2048]{3,2,1,0:T(8,128)(2,1)S(1)}, bf16[2,6,16,2048]{3,2,1,0:T(8,128)(2,1)S(1)}, u32[]{:S(2)}, u32[]{:S(2)}) %collective-permute-start.4) | collective-permute-done | bytes 786464 | tf_op jit(solution)/shard_map/ppermute | solution.py:309
  108.3 1.0 collective-permute-start.7
  109.3 1.5 collective-permute-start.8
  110.8 0.9 collective-permute-start.9
  111.8 0.9 copy-done.12
  112.7 16.8 %block_grads.1 = (bf16[1,2048,2048]{2,1,0:T(8,128)(2,1)}, f32[2,4,128,512]{3,2,1,0:T(8,128)}, bf16[2,4,128,512]{3,2,1,0:T(8,128)(2,1)}) custom-call(s32[2]{0:T(128)} %pad_add_fusion.me_ref, bf16[4,512,512]{2,1,0:T(8,128)(2,1)} %f_ref.3, bf16[1,2048,2048]{2,1,0:T(8,128)(2,1)} %x_ref.3, bf16[8,2,2,16,2048]{4,3,2,1,0:T(8,128)(2,1)} %copy-done, ...), custom_call_target="tpu_custom_call" | custom-call | flops 8589934592 | bytes 25165824 | tf_op jit(solution)/shard_map/block_grads/pallas_call | solution.py:198
  129.5 0.3 collective-permute-done.7.rest_1_
  129.8 16.1 %collective-permute-done.8.rest_2_ = bf16[2,6,16,2048]{3,2,1,0:T(8,128)(2,1)} collective-permute-done((bf16[2,6,16,2048]{3,2,1,0:T(8,128)(2,1)}, bf16[2,6,16,2048]{3,2,1,0:T(8,128)(2,1)}, u32[]{:S(2)}, u32[]{:S(2)}) %collective-permute-start.8) | collective-permute-done | bytes 786464 | tf_op jit(solution)/shard_map/ppermute | solution.py:309
  146.1 1.6 collective-permute-start.21
  147.7 0.8 collective-permute-start.16
  148.5 1.9 collective-permute-start.17
  150.4 0.6 collective-permute-start.19
  151.0 20.3 %collective-permute-done.21 = bf16[2,4,128,512]{3,2,1,0:T(8,128)(2,1)S(1)} collective-permute-done((bf16[2,4,128,512]{3,2,1,0:T(8,128)(2,1)}, bf16[2,4,128,512]{3,2,1,0:T(8,128)(2,1)S(1)}, u32[]{:S(2)}, u32[]{:S(2)}) %collective-permute-start.21) | collective-permute-done | bytes 1048608 | tf_op jit(solution)/shard_map/ppermute | solution.py:314
  171.3 1.6 collective-permute-start.10
  172.9 2.0 convert_add_fusion
  175.0 1.6 collective-permute-start.11
  176.6 8.8 %collective-permute-done.17.rest_5_ = bf16[2,6,16,2048]{3,2,1,0:T(8,128)(2,1)} collective-permute-done((bf16[2,6,16,2048]{3,2,1,0:T(8,128)(2,1)}, bf16[2,6,16,2048]{3,2,1,0:T(8,128)(2,1)}, u32[]{:S(2)}, u32[]{:S(2)}) %collective-permute-start.17) | collective-permute-done | bytes 786464 | tf_op jit(solution)/shard_map/ppermute | solution.py:309
  185.4 1.5 collective-permute-start.12
  186.9 1.1 collective-permute-start.13
  187.9 2.6 %collective-permute-start.22 = (bf16[1,4,128,512]{3,2,1,0:T(8,128)(2,1)S(1)}, bf16[1,4,128,512]{3,2,1,0:T(8,128)(2,1)S(1)}, u32[]{:S(2)}, u32[]{:S(2)}) collective-permute-start(bf16[1,4,128,512]{3,2,1,0:T(8,128)(2,1)S(1)} %slice.21), channel_id=1, source_target_pairs={{0,16},{8,24},{16,0},{24,8},{1,17},{9,25},{17,1},{25,9},{2,18},{10... | collective-permute-start | bytes 1572872 | tf_op jit(solution)/shard_map/ppermute | solution.py:314
  190.5 12.4 %mixed.2 = (bf16[1,2048,2048]{2,1,0:T(8,128)(2,1)}, bf16[4,8,16,128]{3,2,1,0:T(8,128)(2,1)}) custom-call(s32[2]{0:T(128)} %pad_add_fusion.me_ref, bf16[2048,32]{1,0:T(8,128)(2,1)} %bitcast.11, bf16[1,2048,2048]{2,1,0:T(8,128)(2,1)} %gate_ref.7, bf16[1,2048,2048]{2,1,0:T(8,128)(2,1)} %cot_ref.7, bf16[2,6,16,2048]{3,2,1,0:T(8,128)(2,1)} %get-tuple-element.145.rest_0_, ...), custom_call_target="tpu_custom_call" | custom-call | flops 3221225472 | bytes 25165824 | tf_op jit(solution)/shard_map/mixed/pallas_call | solution.py:272
  203.0 0.5 collective-permute-start.14
  203.4 1.4 collective-permute-start.15
  205.0 6.5 %collective-permute-done.14.rest_5_ = bf16[2,2,16,2048]{3,2,1,0:T(8,128)(2,1)} collective-permute-done((bf16[2,2,16,2048]{3,2,1,0:T(8,128)(2,1)}, bf16[2,2,16,2048]{3,2,1,0:T(8,128)(2,1)}, u32[]{:S(2)}, u32[]{:S(2)}) %collective-permute-start.14) | collective-permute-done | bytes 262176 | tf_op jit(solution)/shard_map/ppermute | solution.py:309
  211.6 0.3 collective-permute-done.15.rest_6_
  211.9 5.8 %mixed.3 = (bf16[1,2048,2048]{2,1,0:T(8,128)(2,1)}, bf16[4,8,16,128]{3,2,1,0:T(8,128)(2,1)}) custom-call(s32[2]{0:T(128)} %pad_add_fusion.me_ref, bf16[2048,32]{1,0:T(8,128)(2,1)} %bitcast.12, bf16[1,2048,2048]{2,1,0:T(8,128)(2,1)} %gate_ref.7, bf16[1,2048,2048]{2,1,0:T(8,128)(2,1)} %cot_ref.7, ...), custom_call_target="tpu_custom_call", output_to_operand_aliasing={{0}: (12, {}), {1}: (13, {})} | custom-call | flops 1073741824 | bytes 8388608 | tf_op jit(solution)/shard_map/mixed/pallas_call | solution.py:272
  217.7 3.3 %all-to-all-start.1 = ((bf16[4,8,16,128]{3,2,1,0:T(8,128)(2,1)}), bf16[4,8,16,128]{3,2,1,0:T(8,128)(2,1)S(1)}, u32[]{:S(2)}, u32[]{:S(2)}) async-start(bf16[4,8,16,128]{3,2,1,0:T(8,128)(2,1)} %get-tuple-element.165), calls=%async_computation.1 | async-start | bytes 262144 | tf_op jit(solution)/shard_map/all_to_all | solution.py:336
  221.0 1.2 fusion
  222.2 5.3 %all-to-all-done.1 = bf16[4,8,16,128]{3,2,1,0:T(8,128)(2,1)S(1)} async-done(((bf16[4,8,16,128]{3,2,1,0:T(8,128)(2,1)}), bf16[4,8,16,128]{3,2,1,0:T(8,128)(2,1)S(1)}, u32[]{:S(2)}, u32[]{:S(2)}) %all-to-all-start.1) | async-done | bytes 131104 | tf_op jit(solution)/shard_map/all_to_all | solution.py:336
  227.7 0.4 copy.21
  228.1 0.3 reshape.23
  228.4 0.8 copy.22
  (46 shorter events, 0.8 us)
Async XLA Ops:
  7.4 5.3 %copy-start.1 = (bf16[64,32,32]{0,2,1:T(8,128)(2,1)S(1)}, bf16[64,32,32]{0,2,1:T(8,128)(2,1)}, u32[]{:S(2)}) copy-start(bf16[64,32,32]{0,2,1:T(8,128)(2,1)} %param.10) | copy-start | bytes 393220
  7.4 32.0 %all-to-all-start = ((bf16[8,2,2,16,2048]{4,3,2,1,0:T(8,128)(2,1)}), bf16[8,2,2,16,2048]{4,3,2,1,0:T(8,128)(2,1)S(1)}, u32[]{:S(2)}, u32[]{:S(2)}) async-start(bf16[8,2,2,16,2048]{4,3,2,1,0:T(8,128)(2,1)} %hidden_grad.2.rest_0_), calls=%async_computation | async-start | bytes 4194304 | tf_op jit(solution)/shard_map/all_to_all | solution.py:359
  25.3 17.5 %copy-start.6 = (bf16[2,6,16,2048]{3,2,1,0:T(8,128)(2,1)S(1)}, bf16[2,6,16,2048]{3,2,1,0:T(8,128)(2,1)}, u32[]{:S(2)}) copy-start(bf16[2,6,16,2048]{3,2,1,0:T(8,128)(2,1)} %get-tuple-element.117) | copy-start | bytes 2359300
  39.4 73.3 %copy-start = (bf16[8,2,2,16,2048]{4,3,2,1,0:T(8,128)(2,1)}, bf16[8,2,2,16,2048]{4,3,2,1,0:T(8,128)(2,1)S(1)}, u32[]{:S(2)}) copy-start(bf16[8,2,2,16,2048]{4,3,2,1,0:T(8,128)(2,1)S(1)} %all-to-all-done.hg_ref) | copy-start | bytes 6291460
  39.4 21.6 %collective-permute-start = (bf16[2,6,16,2048]{3,2,1,0:T(8,128)(2,1)}, bf16[2,6,16,2048]{3,2,1,0:T(8,128)(2,1)S(1)}, u32[]{:S(2)}, u32[]{:S(2)}) collective-permute-start(bf16[2,6,16,2048]{3,2,1,0:T(8,128)(2,1)} %get-tuple-element.113), channel_id=1, source_target_pairs={{0,6},{1,7},{2,4},{3,5},{4,2},{5,3},{6,0},{7,1},{8,14},{9,15},{10,... | collective-permute-start | bytes 2359304 | tf_op jit(solution)/shard_map/ppermute | solution.py:309
  40.0 37.9 %collective-permute-start.1 = (bf16[2,6,16,2048]{3,2,1,0:T(8,128)(2,1)}, bf16[2,6,16,2048]{3,2,1,0:T(8,128)(2,1)S(1)}, u32[]{:S(2)}, u32[]{:S(2)}) collective-permute-start(bf16[2,6,16,2048]{3,2,1,0:T(8,128)(2,1)} %get-tuple-element.114), channel_id=1, source_target_pairs={{0,4},{1,5},{2,6},{3,7},{4,0},{5,1},{6,2},{7,3},{8,12},{9,13},{10,... | collective-permute-start | bytes 2359304 | tf_op jit(solution)/shard_map/ppermute | solution.py:309
  41.4 36.6 %collective-permute-start.2 = (bf16[2,6,16,2048]{3,2,1,0:T(8,128)(2,1)}, bf16[2,6,16,2048]{3,2,1,0:T(8,128)(2,1)S(1)}, u32[]{:S(2)}, u32[]{:S(2)}) collective-permute-start(bf16[2,6,16,2048]{3,2,1,0:T(8,128)(2,1)} %get-tuple-element.115), channel_id=1, source_target_pairs={{0,2},{1,3},{2,0},{3,1},{4,6},{5,7},{6,4},{7,5},{8,10},{9,11},{10,... | collective-permute-start | bytes 2359304 | tf_op jit(solution)/shard_map/ppermute | solution.py:309
  42.9 49.1 %collective-permute-start.3 = (bf16[2,6,16,2048]{3,2,1,0:T(8,128)(2,1)}, bf16[2,6,16,2048]{3,2,1,0:T(8,128)(2,1)S(1)}, u32[]{:S(2)}, u32[]{:S(2)}) collective-permute-start(bf16[2,6,16,2048]{3,2,1,0:T(8,128)(2,1)} %get-tuple-element.116), channel_id=1, source_target_pairs={{0,7},{1,6},{2,5},{3,4},{4,3},{5,2},{6,1},{7,0},{8,15},{9,14},{10,... | collective-permute-start | bytes 2359304 | tf_op jit(solution)/shard_map/ppermute | solution.py:309
  42.9 65.4 %collective-permute-start.4 = (bf16[2,6,16,2048]{3,2,1,0:T(8,128)(2,1)S(1)}, bf16[2,6,16,2048]{3,2,1,0:T(8,128)(2,1)S(1)}, u32[]{:S(2)}, u32[]{:S(2)}) collective-permute-start(bf16[2,6,16,2048]{3,2,1,0:T(8,128)(2,1)S(1)} %copy-done.6), channel_id=1, source_target_pairs={{0,5},{1,4},{2,7},{3,6},{4,1},{5,0},{6,3},{7,2},{8,13},{9,12},{10,... | collective-permute-start | bytes 2359304 | tf_op jit(solution)/shard_map/ppermute | solution.py:309
  61.0 47.3 %copy-start.7 = (bf16[2,6,16,2048]{3,2,1,0:T(8,128)(2,1)}, bf16[2,6,16,2048]{3,2,1,0:T(8,128)(2,1)S(1)}, u32[]{:S(2)}) copy-start(bf16[2,6,16,2048]{3,2,1,0:T(8,128)(2,1)S(1)} %collective-permute-done.rest_1_) | copy-start | bytes 2359300
  61.0 50.8 %collective-permute-start.5 = (bf16[2,6,16,2048]{3,2,1,0:T(8,128)(2,1)}, bf16[2,6,16,2048]{3,2,1,0:T(8,128)(2,1)S(1)}, u32[]{:S(2)}, u32[]{:S(2)}) collective-permute-start(bf16[2,6,16,2048]{3,2,1,0:T(8,128)(2,1)} %get-tuple-element.123), channel_id=1, source_target_pairs={{0,3},{1,2},{2,1},{3,0},{4,7},{5,6},{6,5},{7,4},{8,11},{9,10},{10,... | collective-permute-start | bytes 2359304 | tf_op jit(solution)/shard_map/ppermute | solution.py:309
  77.9 31.4 %copy-start.8 = (bf16[2,6,16,2048]{3,2,1,0:T(8,128)(2,1)}, bf16[2,6,16,2048]{3,2,1,0:T(8,128)(2,1)S(1)}, u32[]{:S(2)}) copy-start(bf16[2,6,16,2048]{3,2,1,0:T(8,128)(2,1)S(1)} %collective-permute-done.1.rest_2_) | copy-start | bytes 2359300
  77.9 34.8 %collective-permute-start.6 = (bf16[2,6,16,2048]{3,2,1,0:T(8,128)(2,1)}, bf16[2,6,16,2048]{3,2,1,0:T(8,128)(2,1)}, u32[]{:S(2)}, u32[]{:S(2)}) collective-permute-start(bf16[2,6,16,2048]{3,2,1,0:T(8,128)(2,1)} %get-tuple-element.124), channel_id=1, source_target_pairs={{0,1},{1,0},{2,3},{3,2},{4,5},{5,4},{6,7},{7,6},{8,9},{9,8},{10,11... | collective-permute-start | bytes 2359304 | tf_op jit(solution)/shard_map/ppermute | solution.py:309
  77.9 32.9 %copy-start.9 = (bf16[2,6,16,2048]{3,2,1,0:T(8,128)(2,1)}, bf16[2,6,16,2048]{3,2,1,0:T(8,128)(2,1)S(1)}, u32[]{:S(2)}) copy-start(bf16[2,6,16,2048]{3,2,1,0:T(8,128)(2,1)S(1)} %collective-permute-done.2.rest_3_) | copy-start | bytes 2359300
  92.0 19.8 %copy-start.10 = (bf16[2,6,16,2048]{3,2,1,0:T(8,128)(2,1)}, bf16[2,6,16,2048]{3,2,1,0:T(8,128)(2,1)S(1)}, u32[]{:S(2)}) copy-start(bf16[2,6,16,2048]{3,2,1,0:T(8,128)(2,1)S(1)} %collective-permute-done.3.rest_4_) | copy-start | bytes 2359300
  108.3 3.5 %copy-start.11 = (bf16[2,6,16,2048]{3,2,1,0:T(8,128)(2,1)}, bf16[2,6,16,2048]{3,2,1,0:T(8,128)(2,1)S(1)}, u32[]{:S(2)}) copy-start(bf16[2,6,16,2048]{3,2,1,0:T(8,128)(2,1)S(1)} %collective-permute-done.4.rest_5_) | copy-start | bytes 2359300
  108.3 21.5 %collective-permute-start.7 = (bf16[2,6,16,2048]{3,2,1,0:T(8,128)(2,1)}, bf16[2,6,16,2048]{3,2,1,0:T(8,128)(2,1)S(1)}, u32[]{:S(2)}, u32[]{:S(2)}) collective-permute-start(bf16[2,6,16,2048]{3,2,1,0:T(8,128)(2,1)} %get-tuple-element.134), channel_id=1, source_target_pairs={{0,6},{1,7},{2,4},{3,5},{4,2},{5,3},{6,0},{7,1},{8,14},{9,15},{10,... | collective-permute-start | bytes 2359304 | tf_op jit(solution)/shard_map/ppermute | solution.py:309
  109.3 36.6 %collective-permute-start.8 = (bf16[2,6,16,2048]{3,2,1,0:T(8,128)(2,1)}, bf16[2,6,16,2048]{3,2,1,0:T(8,128)(2,1)}, u32[]{:S(2)}, u32[]{:S(2)}) collective-permute-start(bf16[2,6,16,2048]{3,2,1,0:T(8,128)(2,1)} %get-tuple-element.135), channel_id=1, source_target_pairs={{0,4},{1,5},{2,6},{3,7},{4,0},{5,1},{6,2},{7,3},{8,12},{9,13},{10,... | collective-permute-start | bytes 2359304 | tf_op jit(solution)/shard_map/ppermute | solution.py:309
  110.8 35.3 %collective-permute-start.9 = (bf16[2,6,16,2048]{3,2,1,0:T(8,128)(2,1)}, bf16[2,6,16,2048]{3,2,1,0:T(8,128)(2,1)}, u32[]{:S(2)}, u32[]{:S(2)}) collective-permute-start(bf16[2,6,16,2048]{3,2,1,0:T(8,128)(2,1)} %get-tuple-element.136), channel_id=1, source_target_pairs={{0,2},{1,3},{2,0},{3,1},{4,6},{5,7},{6,4},{7,5},{8,10},{9,11},{10,... | collective-permute-start | bytes 2359304 | tf_op jit(solution)/shard_map/ppermute | solution.py:309
  111.8 0.9 copy-start.12
  129.8 45.1 %copy-start.2 = (bf16[2,6,16,2048]{3,2,1,0:T(8,128)(2,1)}, bf16[2,6,16,2048]{3,2,1,0:T(8,128)(2,1)S(1)}, u32[]{:S(2)}) copy-start(bf16[2,6,16,2048]{3,2,1,0:T(8,128)(2,1)S(1)} %collective-permute-done.7.rest_1_) | copy-start | bytes 2359300
  146.1 25.1 %collective-permute-start.21 = (bf16[2,4,128,512]{3,2,1,0:T(8,128)(2,1)}, bf16[2,4,128,512]{3,2,1,0:T(8,128)(2,1)S(1)}, u32[]{:S(2)}, u32[]{:S(2)}) collective-permute-start(bf16[2,4,128,512]{3,2,1,0:T(8,128)(2,1)} %get-tuple-element.156.rest_8_), channel_id=1, source_target_pairs={{0,8},{8,0},{16,24},{24,16},{1,9},{9,1},{17,25},{25,17},{2,10},{10... | collective-permute-start | bytes 3145736 | tf_op jit(solution)/shard_map/ppermute | solution.py:314
  147.7 27.3 %collective-permute-start.16 = (bf16[2,6,16,2048]{3,2,1,0:T(8,128)(2,1)}, bf16[2,6,16,2048]{3,2,1,0:T(8,128)(2,1)}, u32[]{:S(2)}, u32[]{:S(2)}) collective-permute-start(bf16[2,6,16,2048]{3,2,1,0:T(8,128)(2,1)} %get-tuple-element.152), channel_id=1, source_target_pairs={{0,7},{1,6},{2,5},{3,4},{4,3},{5,2},{6,1},{7,0},{8,15},{9,14},{10,... | collective-permute-start | bytes 2359304 | tf_op jit(solution)/shard_map/ppermute | solution.py:309
  148.5 36.9 %collective-permute-start.17 = (bf16[2,6,16,2048]{3,2,1,0:T(8,128)(2,1)}, bf16[2,6,16,2048]{3,2,1,0:T(8,128)(2,1)}, u32[]{:S(2)}, u32[]{:S(2)}) collective-permute-start(bf16[2,6,16,2048]{3,2,1,0:T(8,128)(2,1)} %get-tuple-element.153), channel_id=1, source_target_pairs={{0,5},{1,4},{2,7},{3,6},{4,1},{5,0},{6,3},{7,2},{8,13},{9,12},{10,... | collective-permute-start | bytes 2359304 | tf_op jit(solution)/shard_map/ppermute | solution.py:309
  150.4 36.5 %collective-permute-start.18 = (bf16[2,6,16,2048]{3,2,1,0:T(8,128)(2,1)}, bf16[2,6,16,2048]{3,2,1,0:T(8,128)(2,1)}, u32[]{:S(2)}, u32[]{:S(2)}) collective-permute-start(bf16[2,6,16,2048]{3,2,1,0:T(8,128)(2,1)} %get-tuple-element.154), channel_id=1, source_target_pairs={{0,3},{1,2},{2,1},{3,0},{4,7},{5,6},{6,5},{7,4},{8,11},{9,10},{10,... | collective-permute-start | bytes 2359304 | tf_op jit(solution)/shard_map/ppermute | solution.py:309
  150.4 37.5 %collective-permute-start.19 = (bf16[2,6,16,2048]{3,2,1,0:T(8,128)(2,1)}, bf16[2,6,16,2048]{3,2,1,0:T(8,128)(2,1)}, u32[]{:S(2)}, u32[]{:S(2)}) collective-permute-start(bf16[2,6,16,2048]{3,2,1,0:T(8,128)(2,1)} %get-tuple-element.155), channel_id=1, source_target_pairs={{0,1},{1,0},{2,3},{3,2},{4,5},{5,4},{6,7},{7,6},{8,9},{9,8},{10,11... | collective-permute-start | bytes 2359304 | tf_op jit(solution)/shard_map/ppermute | solution.py:309
  171.3 31.7 %collective-permute-start.10 = (bf16[2,2,16,2048]{3,2,1,0:T(8,128)(2,1)}, bf16[2,2,16,2048]{3,2,1,0:T(8,128)(2,1)S(1)}, u32[]{:S(2)}, u32[]{:S(2)}) collective-permute-start(bf16[2,2,16,2048]{3,2,1,0:T(8,128)(2,1)} %get-tuple-element.138), channel_id=1, source_target_pairs={{0,6},{1,7},{2,4},{3,5},{4,2},{5,3},{6,0},{7,1},{8,14},{9,15},{10,... | collective-permute-start | bytes 786440 | tf_op jit(solution)/shard_map/ppermute | solution.py:309
  175.0 28.5 %collective-permute-start.11 = (bf16[2,2,16,2048]{3,2,1,0:T(8,128)(2,1)}, bf16[2,2,16,2048]{3,2,1,0:T(8,128)(2,1)S(1)}, u32[]{:S(2)}, u32[]{:S(2)}) collective-permute-start(bf16[2,2,16,2048]{3,2,1,0:T(8,128)(2,1)} %get-tuple-element.139), channel_id=1, source_target_pairs={{0,4},{1,5},{2,6},{3,7},{4,0},{5,1},{6,2},{7,3},{8,12},{9,13},{10,... | collective-permute-start | bytes 786440 | tf_op jit(solution)/shard_map/ppermute | solution.py:309
  185.4 19.5 %collective-permute-start.12 = (bf16[2,2,16,2048]{3,2,1,0:T(8,128)(2,1)}, bf16[2,2,16,2048]{3,2,1,0:T(8,128)(2,1)S(1)}, u32[]{:S(2)}, u32[]{:S(2)}) collective-permute-start(bf16[2,2,16,2048]{3,2,1,0:T(8,128)(2,1)} %get-tuple-element.140), channel_id=1, source_target_pairs={{0,2},{1,3},{2,0},{3,1},{4,6},{5,7},{6,4},{7,5},{8,10},{9,11},{10,... | collective-permute-start | bytes 786440 | tf_op jit(solution)/shard_map/ppermute | solution.py:309
  186.9 18.2 %collective-permute-start.13 = (bf16[2,2,16,2048]{3,2,1,0:T(8,128)(2,1)}, bf16[2,2,16,2048]{3,2,1,0:T(8,128)(2,1)}, u32[]{:S(2)}, u32[]{:S(2)}) collective-permute-start(bf16[2,2,16,2048]{3,2,1,0:T(8,128)(2,1)} %get-tuple-element.141), channel_id=1, source_target_pairs={{0,7},{1,6},{2,5},{3,4},{4,3},{5,2},{6,1},{7,0},{8,15},{9,14},{10,... | collective-permute-start | bytes 786440 | tf_op jit(solution)/shard_map/ppermute | solution.py:309
  187.9 29.8 %collective-permute-start.22 = (bf16[1,4,128,512]{3,2,1,0:T(8,128)(2,1)S(1)}, bf16[1,4,128,512]{3,2,1,0:T(8,128)(2,1)S(1)}, u32[]{:S(2)}, u32[]{:S(2)}) collective-permute-start(bf16[1,4,128,512]{3,2,1,0:T(8,128)(2,1)S(1)} %slice.21), channel_id=1, source_target_pairs={{0,16},{8,24},{16,0},{24,8},{1,17},{9,25},{17,1},{25,9},{2,18},{10... | collective-permute-start | bytes 1572872 | tf_op jit(solution)/shard_map/ppermute | solution.py:314
  203.0 9.0 %copy-start.3 = (bf16[2,2,16,2048]{3,2,1,0:T(8,128)(2,1)}, bf16[2,2,16,2048]{3,2,1,0:T(8,128)(2,1)S(1)}, u32[]{:S(2)}) copy-start(bf16[2,2,16,2048]{3,2,1,0:T(8,128)(2,1)S(1)} %collective-permute-done.10.rest_1_) | copy-start | bytes 786436
  203.0 8.6 %collective-permute-start.14 = (bf16[2,2,16,2048]{3,2,1,0:T(8,128)(2,1)}, bf16[2,2,16,2048]{3,2,1,0:T(8,128)(2,1)}, u32[]{:S(2)}, u32[]{:S(2)}) collective-permute-start(bf16[2,2,16,2048]{3,2,1,0:T(8,128)(2,1)} %get-tuple-element.142), channel_id=1, source_target_pairs={{0,5},{1,4},{2,7},{3,6},{4,1},{5,0},{6,3},{7,2},{8,13},{9,12},{10,... | collective-permute-start | bytes 786440 | tf_op jit(solution)/shard_map/ppermute | solution.py:309
  203.4 8.5 %copy-start.4 = (bf16[2,2,16,2048]{3,2,1,0:T(8,128)(2,1)}, bf16[2,2,16,2048]{3,2,1,0:T(8,128)(2,1)S(1)}, u32[]{:S(2)}) copy-start(bf16[2,2,16,2048]{3,2,1,0:T(8,128)(2,1)S(1)} %collective-permute-done.11.rest_2_) | copy-start | bytes 786436
  203.4 8.5 %collective-permute-start.15 = (bf16[2,2,16,2048]{3,2,1,0:T(8,128)(2,1)}, bf16[2,2,16,2048]{3,2,1,0:T(8,128)(2,1)}, u32[]{:S(2)}, u32[]{:S(2)}) collective-permute-start(bf16[2,2,16,2048]{3,2,1,0:T(8,128)(2,1)} %get-tuple-element.143), channel_id=1, source_target_pairs={{0,3},{1,2},{2,1},{3,0},{4,7},{5,6},{6,5},{7,4},{8,11},{9,10},{10,... | collective-permute-start | bytes 786440 | tf_op jit(solution)/shard_map/ppermute | solution.py:309
  204.9 7.0 %copy-start.5 = (bf16[2,2,16,2048]{3,2,1,0:T(8,128)(2,1)}, bf16[2,2,16,2048]{3,2,1,0:T(8,128)(2,1)S(1)}, u32[]{:S(2)}) copy-start(bf16[2,2,16,2048]{3,2,1,0:T(8,128)(2,1)S(1)} %collective-permute-done.12.rest_3_) | copy-start | bytes 786436
  204.9 7.0 %collective-permute-start.20 = (bf16[2,2,16,2048]{3,2,1,0:T(8,128)(2,1)}, bf16[2,2,16,2048]{3,2,1,0:T(8,128)(2,1)}, u32[]{:S(2)}, u32[]{:S(2)}) collective-permute-start(bf16[2,2,16,2048]{3,2,1,0:T(8,128)(2,1)} %get-tuple-element.158), channel_id=1, source_target_pairs={{0,1},{1,0},{2,3},{3,2},{4,5},{5,4},{6,7},{7,6},{8,9},{9,8},{10,11... | collective-permute-start | bytes 786440 | tf_op jit(solution)/shard_map/ppermute | solution.py:309
  217.7 9.8 %all-to-all-start.1 = ((bf16[4,8,16,128]{3,2,1,0:T(8,128)(2,1)}), bf16[4,8,16,128]{3,2,1,0:T(8,128)(2,1)S(1)}, u32[]{:S(2)}, u32[]{:S(2)}) async-start(bf16[4,8,16,128]{3,2,1,0:T(8,128)(2,1)} %get-tuple-element.165), calls=%async_computation.1 | async-start | bytes 262144 | tf_op jit(solution)/shard_map/all_to_all | solution.py:336
